TPU v7x, 32 devices: a whole 2x2x4 slice. The times are simulated.
32 devices in a mesh: dp: 16 (over z, y, x), tensor: 2 (over core).
Axes of the slice: x: 2, y: 2, z: 4, core: 2. Of those that a mesh axis runs over, the one named last changes fastest.
Arguments:
- hidden_in: bfloat16 [16384, 1536], P('dp'), may hold values from -6 to 6
- out_grad: bfloat16 [16384, 1536], P('dp'), may hold values from -6 to 6
- routes: int32 [16384, 8], P('dp'), may hold values from 0 to 15, all different within a row; in each aligned block of 1024 rows (0 to 1023, 1024 to 2047, ...) at most 768 rows name the same one
- segments: int32 [16384], P('dp'), may hold values from 0 to 60, never falling along the last dimension, each value on 1 to 800 neighbouring positions
- norm_gains: float32 [2, 1536], P(None, 'dp'), may hold values from 0.5 to 1.5
- gains_mean: float32 [2, 1536], P(None, 'dp'), may hold values from -256 to 256
- gains_square: float32 [2, 1536], P(None, 'dp'), may hold values from 3883.008 to 62095.36
- w_query: float32 [1536, 1536], P('dp', 'tensor'), may hold values from -0.5 to 0.5
- query_mean: float32 [1536, 1536], P('dp', 'tensor'), may hold values from -80 to 80
- query_square: float32 [1536, 1536], P('dp', 'tensor'), may hold values from 430.8992 to 6897.664
- key_value_weight: float32 [2, 1536, 512], P(None, 'dp', 'tensor'), may hold values from -0.5 to 0.5
- key_value_first_moment: float32 [2, 1536, 512], P(None, 'dp', 'tensor'), may hold values from -80 to 80
- key_value_second_moment: float32 [2, 1536, 512], P(None, 'dp', 'tensor'), may hold values from 430.8992 to 6897.664
- w_out: float32 [1536, 1536], P('tensor', 'dp'), may hold values from -1.5 to 1.5
- out_mean: float32 [1536, 1536], P('tensor', 'dp'), may hold values from -16 to 16
- out_square: float32 [1536, 1536], P('tensor', 'dp'), may hold values from 13.9264 to 222.8224
- w_router: float32 [1536, 16], P('dp'), may hold values from -0.078125 to 0.078125
- router_mean: float32 [1536, 16], P('dp'), may hold values from -896 to 896
- router_square: float32 [1536, 16], P('dp'), may hold values from 43089.92 to 689766.4
- w_gateup: float32 [16, 2, 1536, 512], P(None, None, 'dp', 'tensor'), may hold values from -0.15625 to 0.15625
- gateup_mean: float32 [16, 2, 1536, 512], P(None, None, 'dp', 'tensor'), may hold values from -32 to 32
- gateup_square: float32 [16, 2, 1536, 512], P(None, None, 'dp', 'tensor'), may hold values from 52.4288 to 851.968
- w_down: float32 [16, 512, 1536], P(None, 'tensor', 'dp'), may hold values from -4 to 4
- down_mean: float32 [16, 512, 1536], P(None, 'tensor', 'dp'), may hold values from -1 to 1
- down_square: float32 [16, 512, 1536], P(None, 'tensor', 'dp'), may hold values from 0.0589824 to 0.950272
Outputs:
- block_out: bfloat16 [16384, 1536], P('dp')
- input_grad: float32 [16384, 1536], P('dp')
- gains_mean_new: float32 [2, 1536], P(None, 'dp')
- gains_square_new: float32 [2, 1536], P(None, 'dp')
- gains_new: float32 [2, 1536], P(None, 'dp')
- query_mean_new: float32 [1536, 1536], P('dp', 'tensor')
- query_square_new: float32 [1536, 1536], P('dp', 'tensor')
- query_new: float32 [1536, 1536], P('dp', 'tensor')
- keyval_mean_new: float32 [2, 1536, 512], P(None, 'dp', 'tensor')
- keyval_square_new: float32 [2, 1536, 512], P(None, 'dp', 'tensor')
- keyval_new: float32 [2, 1536, 512], P(None, 'dp', 'tensor')
- out_mean_new: float32 [1536, 1536], P('tensor', 'dp')
- out_square_new: float32 [1536, 1536], P('tensor', 'dp')
- out_new: float32 [1536, 1536], P('tensor', 'dp')
- router_mean_new: float32 [1536, 16], P('dp')
- router_square_new: float32 [1536, 16], P('dp')
- router_new: float32 [1536, 16], P('dp')
- gateup_mean_new: float32 [16, 2, 1536, 512], P(None, None, 'dp', 'tensor')
- gateup_square_new: float32 [16, 2, 1536, 512], P(None, None, 'dp', 'tensor')
- gateup_new: float32 [16, 2, 1536, 512], P(None, None, 'dp', 'tensor')
- down_mean_new: float32 [16, 512, 1536], P(None, 'tensor', 'dp')
- down_square_new: float32 [16, 512, 1536], P(None, 'tensor', 'dp')
- down_new: float32 [16, 512, 1536], P(None, 'tensor', 'dp')
Inputs may be any that keep to these rules, and one draw needn't show every extreme that they name: `routes`: each row names 8 different experts. Among the rows of one device (each aligned block of 1024 rows) no expert is named by more than 768 rows, a bound that some block reaches. `segments`: ids never fall along the array; each id covers 1 to 800 positions, and one covers exactly 800.
All inputs are finite; a program needn't handle non-finite values.
Results may differ from a plain program's by a relative error of at most 0.018.
The roundings to bfloat16 on the way count: a program that leaves them out, or rounds other values in their place, can miss the bound.
Values may be sent and summed in bfloat16 or wider, within the bound.
A program may use at most 384 MiB of HBM per device.

v0:
```python
import functools

import jax
import jax.numpy as jnp
from jax import lax
from jax.experimental import pallas as pl
from jax.experimental.pallas import tpu as pltpu
from jax.sharding import PartitionSpec as P

MODEL_DIM = 1536
QUERY_HEADS = 24
HEAD_DIM = 64
F = 512
SEQUENCE_LENGTH = 1024
STEP = 10

NORM_EPSILON = 1e-06
SCORE_SCALE = 0.015625
RESIDUAL_SCALE = 0.22
ROPE_BASE = 10000.0
FIRST_DECAY = 0.9
SECOND_DECAY = 0.95
ADAM_EPSILON = 1e-08
WEIGHT_DECAY = 0.1
GAIN_RATE = 0.6
MASK_VALUE = -1e30
HIGHEST_PRECISION = lax.Precision.HIGHEST

BF16 = jnp.bfloat16
F32 = jnp.float32
LANES = 128
ROWS = 256
VMEM_BYTES = 58 * 1024 * 1024

NN = (((1,), (0,)), ((), ()))
NT = (((1,), (1,)), ((), ()))
TN = (((0,), (0,)), ((), ()))


def dot(a, b, dims=NN):
    return lax.dot_general(a, b, dims, preferred_element_type=F32)


def seq_positions(segment_row):
    counter = jnp.arange(segment_row.shape[0], dtype=jnp.int32)
    earlier = jnp.concatenate([segment_row[:1] - 1, segment_row[:-1]])
    starts = lax.cummax(jnp.where(segment_row != earlier, counter, 0), axis=0)
    return counter - starts


def rope_tables(positions):
    half_width = HEAD_DIM // 2
    frequency = ROPE_BASE ** (-2.0 * jnp.arange(half_width, dtype=F32) / HEAD_DIM)
    angles = positions.astype(F32)[:, None] * frequency[None, :]
    cosine, sine = jnp.cos(angles), jnp.sin(angles)
    return (
        jnp.concatenate([cosine] * 4, axis=1),
        jnp.concatenate([-sine, sine] * 2, axis=1),
    )


def rotate_halves(slab):
    lane = lax.broadcasted_iota(jnp.int32, slab.shape, 1)
    ahead = pltpu.roll(slab, LANES - HEAD_DIM // 2, 1)
    behind = pltpu.roll(slab, HEAD_DIM // 2, 1)
    return jnp.where(lane % HEAD_DIM < HEAD_DIM // 2, ahead, behind)


def few_rows(count, base=None):
    for r in range(0, count, 16):
        yield pl.ds(r, 16) if base is None else pl.ds(pl.multiple_of(base + r, 16), 16)


def half_mask(rows, upper):
    lane = lax.broadcasted_iota(jnp.int32, (rows, LANES), 1)
    return (lane >= HEAD_DIM) if upper else (lane < HEAD_DIM)


def spread_heads(slab, lower_out, upper_out, index):
    rows = slab.shape[0]
    moved = pltpu.roll(slab.astype(F32), HEAD_DIM, 1).astype(BF16)
    zero = jnp.zeros_like(slab)
    low, high = half_mask(rows, False), half_mask(rows, True)
    lower_out[index] = jnp.where(low, slab, zero)
    upper_out[index] = jnp.where(high, moved, zero)
    lower_out[index + 1] = jnp.where(low, moved, zero)
    upper_out[index + 1] = jnp.where(high, slab, zero)


def fill_bias(bias, seg_col, seg_row):
    span = bias.shape[0]
    for at in range(0, span, ROWS):
        rows_at = at + lax.broadcasted_iota(jnp.int32, (ROWS, span), 0)
        cols_at = lax.broadcasted_iota(jnp.int32, (ROWS, span), 1)
        allowed = (rows_at >= cols_at) & (seg_col[at : at + ROWS, :] == seg_row[...])
        bias[at : at + ROWS, :] = jnp.where(allowed, 0.0, MASK_VALUE).astype(F32)


def with_earlier(kernel, inputs, count):
    def run(*refs):
        kernel(*refs[:inputs], *refs[inputs + count :])

    return run


def any_specs(arrays):
    return [pl.BlockSpec(memory_space=pl.ANY)] * len(arrays)


def attention_forward_kernel(
    lin_ref, kv_ref, cos_ref, sin_ref, seg_col, seg_row,
    out_ref, q_ref, k_ref, v_ref, lse_ref,
    bias, k_low, k_high, v_low, v_high,
):
    slab_at = pl.program_id(0)
    span = lin_ref.shape[0]
    kv_slabs = kv_ref.shape[1] // (2 * LANES)

    @pl.when(slab_at == 0)
    def _():
        fill_bias(bias, seg_col, seg_row)
        for j in range(kv_slabs):
            lanes = slice(j * LANES, (j + 1) * LANES)
            lin = kv_ref[:, lanes]
            keys = (lin * cos_ref[...] + rotate_halves(lin) * sin_ref[...]).astype(BF16)
            k_ref[:, lanes] = keys
            spread_heads(keys, k_low, k_high, 2 * j)
            lanes = slice((kv_slabs + j) * LANES, (kv_slabs + j + 1) * LANES)
            values = kv_ref[:, lanes].astype(BF16)
            v_ref[:, slice(j * LANES, (j + 1) * LANES)] = values
            spread_heads(values, v_low, v_high, 2 * j)

    lin = lin_ref[...]
    q_ref[...] = (lin * cos_ref[...] + rotate_halves(lin) * sin_ref[...]).astype(BF16)
    kv_even, kv_odd = (2 * slab_at) // 3, (2 * slab_at + 1) // 3
    for at in range(0, span, ROWS):
        rows = slice(at, at + ROWS)
        queries = q_ref[rows, :]
        total = None
        stats = []
        for keys, values, kv_at in ((k_low, v_low, kv_even), (k_high, v_high, kv_odd)):
            upto = at + ROWS
            scores = dot(queries, keys[kv_at, :upto, :], NT) * SCORE_SCALE + bias[rows, :upto]
            highest = jnp.max(scores, axis=1, keepdims=True)
            weights = jnp.exp(scores - highest)
            summed = jnp.sum(weights, axis=1, keepdims=True)
            probability = (weights * (1.0 / summed)).astype(BF16)
            part = dot(probability, values[kv_at, :upto, :])
            total = part if total is None else total + part
            stats.append(highest + jnp.log(summed))
        out_ref[rows, :] = total.astype(BF16)
        spread = jnp.where(half_mask(ROWS, False), stats[0], stats[1])
        turned = spread.T
        lse_ref[0, 0:1, rows] = turned[0:1, :]
        lse_ref[0, 1:2, rows] = turned[HEAD_DIM : HEAD_DIM + 1, :]


def attention_forward(qkv_lin, cosine, sine, segment_row, earlier=()):
    span = qkv_lin.shape[0]
    q_width = MODEL_DIM // 2
    kv_width = (qkv_lin.shape[1] - q_width) // 2
    slabs, kv_heads = q_width // LANES, kv_width // HEAD_DIM
    whole = lambda shape: pl.BlockSpec(shape, lambda g: (0,) * len(shape))
    slab = pl.BlockSpec((span, LANES), lambda g: (0, g))
    q_lin, kv_lin = qkv_lin[:, :q_width], qkv_lin[:, q_width:]
    return pl.pallas_call(
        with_earlier(attention_forward_kernel, 6, len(earlier)),
        grid=(slabs,),
        in_specs=[
            slab, whole((span, 2 * kv_width)), whole((span, LANES)), whole((span, LANES)),
            whole((span, 1)), whole((1, span)),
        ]
        + any_specs(earlier),
        out_specs=[
            slab, slab, whole((span, kv_width)), whole((span, kv_width)),
            pl.BlockSpec((1, 8, span), lambda g: (g, 0, 0)),
        ],
        out_shape=[
            jax.ShapeDtypeStruct((span, q_width), BF16),
            jax.ShapeDtypeStruct((span, q_width), BF16),
            jax.ShapeDtypeStruct((span, kv_width), BF16),
            jax.ShapeDtypeStruct((span, kv_width), BF16),
            jax.ShapeDtypeStruct((slabs, 8, span), F32),
        ],
        scratch_shapes=[pltpu.VMEM((span, span), F32)]
        + [pltpu.VMEM((kv_heads, span, LANES), BF16)] * 4,
        compiler_params=pltpu.CompilerParams(vmem_limit_bytes=VMEM_BYTES),
        cost_estimate=pl.CostEstimate(
            flops=32 * slabs * span * span * LANES, bytes_accessed=16 * span * q_width,
            transcendentals=slabs * span * span,
        ),
        name="attention_forward",
    )(q_lin, kv_lin, cosine, sine, segment_row[:, None], segment_row[None, :], *earlier)


def attention_backward_kernel(
    q_ref, k_ref, v_ref, out_ref, grad_ref, cos_ref, sin_ref, seg_col, seg_row, lse_ref,
    dq_ref, dkv_ref,
    bias, k_low, k_high, v_low, v_high, dk_low, dk_high, dv_low, dv_high, dq_sum,
):
    slab_at = pl.program_id(0)
    span = q_ref.shape[0]
    kv_slabs = k_ref.shape[1] // LANES

    @pl.when(slab_at == 0)
    def _():
        for at in range(0, span, ROWS):
            keys_at = at + lax.broadcasted_iota(jnp.int32, (ROWS, span), 0)
            rows_at = lax.broadcasted_iota(jnp.int32, (ROWS, span), 1)
            allowed = (rows_at >= keys_at) & (seg_col[at : at + ROWS, :] == seg_row[...])
            bias[at : at + ROWS, :] = jnp.where(allowed, 0.0, MASK_VALUE).astype(F32)
        for j in range(kv_slabs):
            lanes = slice(j * LANES, (j + 1) * LANES)
            spread_heads(k_ref[:, lanes], k_low, k_high, 2 * j)
            spread_heads(v_ref[:, lanes], v_low, v_high, 2 * j)
        for sums in (dk_low, dk_high, dv_low, dv_high):
            sums[...] = jnp.zeros_like(sums)

    kv_even, kv_odd = (2 * slab_at) // 3, (2 * slab_at + 1) // 3
    for at in range(0, span, ROWS):
        rows = slice(at, at + ROWS)
        upto = at + ROWS
        queries, grads = q_ref[rows, :], grad_ref[rows, :]
        turned = (grads.astype(F32) * out_ref[rows, :].astype(F32)).T
        zero = jnp.zeros_like(queries)
        dq_part = None
        for upper, keys, values, dk_sum, dv_sum, kv_at in (
            (False, k_low, v_low, dk_low, dv_low, kv_even),
            (True, k_high, v_high, dk_high, dv_high, kv_odd),
        ):
            first = HEAD_DIM if upper else 0
            delta = jnp.sum(turned[first : first + HEAD_DIM, :], axis=0, keepdims=True)
            head = 1 if upper else 0
            total = lse_ref[0, head : head + 1, rows]
            keys_here = keys[kv_at, :upto, :]
            scores = dot(keys_here, queries, NT) * SCORE_SCALE + bias[:upto, rows]
            probability = jnp.exp(scores - total)
            prob_grad = dot(values[kv_at, :upto, :], grads, NT)
            score_grad = (probability * (prob_grad - delta)).astype(BF16)
            mask = half_mask(ROWS, upper)
            dv_sum[kv_at, :upto, :] += dot(
                probability.astype(BF16), jnp.where(mask, grads, zero)
            )
            dk_sum[kv_at, :upto, :] += dot(score_grad, jnp.where(mask, queries, zero))
            part = dot(score_grad, keys_here, TN)
            dq_part = part if dq_part is None else dq_part + part
        dq_sum[rows, :] = dq_part * SCORE_SCALE
    slab = dq_sum[...]
    dq_ref[...] = (slab * cos_ref[...] - rotate_halves(slab) * sin_ref[...]).astype(BF16)

    @pl.when(slab_at == pl.num_programs(0) - 1)
    def _():
        low = half_mask(span, False)

        def joined(sums_low, sums_high, j):
            one = sums_low[2 * j] + pltpu.roll(sums_high[2 * j], HEAD_DIM, 1)
            two = pltpu.roll(sums_low[2 * j + 1], HEAD_DIM, 1) + sums_high[2 * j + 1]
            return jnp.where(low, one, two)

        for j in range(kv_slabs):
            slab = joined(dk_low, dk_high, j) * SCORE_SCALE
            dkv_ref[:, j * LANES : (j + 1) * LANES] = (
                slab * cos_ref[...] - rotate_halves(slab) * sin_ref[...]
            ).astype(BF16)
            at = (kv_slabs + j) * LANES
            dkv_ref[:, at : at + LANES] = joined(dv_low, dv_high, j).astype(BF16)


def attention_backward(
    queries, keys, values, attended, grad, cosine, sine, segment_row, lse, earlier=()
):
    span, q_width = queries.shape
    kv_width = keys.shape[1]
    slabs, kv_heads = q_width // LANES, kv_width // HEAD_DIM
    whole = lambda shape: pl.BlockSpec(shape, lambda g: (0,) * len(shape))
    slab = pl.BlockSpec((span, LANES), lambda g: (0, g))
    return pl.pallas_call(
        with_earlier(attention_backward_kernel, 10, len(earlier)),
        grid=(slabs,),
        in_specs=[
            slab, whole((span, kv_width)), whole((span, kv_width)), slab, slab,
            whole((span, LANES)), whole((span, LANES)), whole((span, 1)), whole((1, span)),
            pl.BlockSpec((1, 8, span), lambda g: (g, 0, 0)),
        ]
        + any_specs(earlier),
        out_specs=[slab, whole((span, 2 * kv_width))],
        out_shape=[
            jax.ShapeDtypeStruct((span, q_width), BF16),
            jax.ShapeDtypeStruct((span, 2 * kv_width), BF16),
        ],
        scratch_shapes=[pltpu.VMEM((span, span), F32)]
        + [pltpu.VMEM((kv_heads, span, LANES), BF16)] * 4
        + [pltpu.VMEM((kv_heads, span, LANES), F32)] * 4
        + [pltpu.VMEM((span, LANES), F32)],
        compiler_params=pltpu.CompilerParams(vmem_limit_bytes=VMEM_BYTES),
        cost_estimate=pl.CostEstimate(
            flops=40 * slabs * span * span * LANES, bytes_accessed=16 * span * q_width,
            transcendentals=slabs * span * span,
        ),
        name="attention_backward",
    )(
        queries, keys, values, attended, grad, cosine, sine,
        segment_row[:, None], segment_row[None, :], lse, *earlier,
    )


EXPERT_ROWS = 256
EXPERT_VMEM = 63 * 1024 * 1024
SLOTS = 4
Z_FROM = (0, -1, 1, 2)
CHUNK = 2
LATE = 2
SENT = 2
MESH_ID = pl.DeviceIdType.MESH


def experts_kernel(
    inner, chunks, row_steps, x_ref, og_ref, xt_ref, ogt_ref, combine_ref,
    pairs_ref, near_ref, far_ref,
    dx_own, dx_twin, dx_other, mix_out, gate_out, *refs,
):
    keep_outs, refs = refs[:SENT], refs[SENT:]
    part_outs, refs = refs[:SENT], refs[SENT:]
    near_outs, refs = refs[: chunks - SENT], refs[chunks - SENT :]
    late_out, first_out, far_out, refs = *refs[:3], refs[3:]
    slots, arrived, held_both, held_down, dx_sum, mix_sum, twin_rows, twin_mix = refs[:8]
    gates, gate_kept, gate_got, gate_full, gate_twin, send, recv, local = refs[8:]
    weights, grads = slots.at[pl.ds(1, chunks)], slots
    near = Neighbours(inner)
    copies = Copies(send, recv, local)
    z, y, x, core, spots = near.z, near.y, near.x, near.core, near.spots
    step = pl.program_id(0)
    steps = row_steps + SLOTS
    chunk, turn = step // steps, step % steps
    last = chunks - 1
    width = x_ref.shape[1]
    block = width // 16
    hidden = held_down.shape[1] // CHUNK
    both = 2 * hidden * CHUNK
    lane = lax.broadcasted_iota(jnp.int32, (EXPERT_ROWS, LANES), 1)
    tokens = dx_sum.shape[0] // 2
    tiles = tokens // EXPERT_ROWS
    tile = (turn + tiles) % row_steps
    rows = pl.ds(pl.multiple_of(tile * EXPERT_ROWS, EXPERT_ROWS), EXPERT_ROWS)

    def near_piece(c, k):
        return pairs_ref.at[c] if k == 0 else near_ref.at[c, k - 1]

    def near_copy(c, k):
        copies.copy(
            lambda c=c, k=k: (near_piece(c, k), weights.at[c, spots[k], y]), ("near", c, k), False
        )

    def near_wait(c, k):
        copies.wait_copy(
            lambda c=c, k=k: (near_piece(c, k), weights.at[c, spots[k], y]), ("near", c, k)
        )

    def far_ends(c, k):
        return far_ref.at[c, k], weights.at[c, spots[k], 1 - y]

    @pl.when(step == 0)
    def _():
        near.greet()
        gates[...] = jnp.zeros_like(gates)
        for k in range(SLOTS):
            near_copy(0, k)
            copies.copy(lambda k=k: far_ends(0, k), ("far", 0, k), False)
        copies.remote(
            lambda: (pairs_ref.at[last], weights.at[last, z, y]), ("y",), ("y",), near.over_y
        )
        for k in range(1, SLOTS):
            copies.remote(
                lambda: (pairs_ref.at[last], weights.at[last, z, y]),
                ("z", k), ("z", BACK[k]), near.along[k],
            )
        for c in range(LATE, last):
            for k in range(1, SLOTS):
                copies.remote(
                    lambda c=c, k=k: (near_piece(c, k), weights.at[c, spots[k], y]),
                    ("f", c, k), ("f", c, k), near.over_y,
                )
        for c in range(1, chunks):
            for k in range(SLOTS if c < last else 1):
                near_copy(c, k)
                if c < LATE or (c < last and k == 0):
                    copies.copy(lambda c=c, k=k: far_ends(c, k), ("far", c, k), False)

    @pl.when(step == steps)
    def _():
        copies.arrived(weights.at[last, z, 1 - y], ("y",), near.over_y)
        for k in range(1, SLOTS):
            copies.remote(
                lambda: (weights.at[last, z, 1 - y],) * 2,
                ("z2", k), ("z2", BACK[k]), near.along[k],
            )

    for c in range(chunks):

        @pl.when(step == c * steps)
        def _():
            for k in range(SLOTS):
                if c < last or k == 0:
                    near_wait(c, k)
                if c < LATE or (c < last and k == 0):
                    copies.wait_copy(lambda c=c, k=k: far_ends(c, k), ("far", c, k))
                elif c < last:
                    copies.arrived(weights.at[c, spots[k], 1 - y], ("f", c, k), near.over_y)
                elif k > 0:
                    copies.arrived(weights.at[c, spots[k], y], ("z", k), near.along[k])
                    copies.arrived(weights.at[c, spots[k], 1 - y], ("z2", k), near.along[k])

    def add_arrived(c):
        copies.arrived(arrived.at[c], ("sum", c), near.over_y)
        for k in range(SLOTS):
            own = grads.at[c, spots[k], y]
            for here in few_rows(own.shape[0]):
                own[here, :] = (
                    own[here, :].astype(F32) + arrived[c, spots[k], here, :].astype(F32)
                ).astype(BF16)
        copies.copy(lambda c=c: (grads.at[c, z, y], keep_outs[c]), ("keep", c))
        for k in range(1, SLOTS):
            copies.remote(
                lambda c=c, k=k: (grads.at[c, spots[k], y], part_outs[c].at[BACK[k] - 1]),
                ("part", c, k), ("part", c, BACK[k]), near.along[k],
            )

    @pl.when(step == 2 * steps + 3)
    def _():
        add_arrived(0)

    @pl.when(step == 3 * steps + 3)
    def _():
        add_arrived(1)

    @pl.when(turn < row_steps)
    def _():
        for e in range(CHUNK):
            first = 2 * hidden * e
            w_both = weights[chunk, :, :, :, first : first + 2 * hidden].reshape(width, 2 * hidden)
            start = both + hidden * e
            w_down = weights[chunk, :, :, :, start : start + hidden].reshape(width, hidden)
            gate_up = dot(x_ref[...], w_both)
            raw = dot(og_ref[...], w_down) * RESIDUAL_SCALE
            gate, up = gate_up[:, :hidden], gate_up[:, hidden:]
            gate_lane = lax.broadcasted_iota(
                jnp.int32, (EXPERT_ROWS, combine_ref.shape[1]), 1
            )
            column = jnp.sum(
                jnp.where(gate_lane == chunk * CHUNK + e, combine_ref[...], 0.0),
                axis=1, keepdims=True,
            )
            sigmoid = 1.0 / (1.0 + jnp.exp(-gate))
            active = gate * sigmoid
            inner_value = (active * up).astype(BF16).astype(F32)
            held_down[rows, hidden * e : hidden * (e + 1)] = (inner_value * column).astype(BF16)
            gates[rows, :] = jnp.where(
                lane == chunk * CHUNK + e,
                jnp.sum(inner_value * raw, axis=1, keepdims=True),
                gates[rows, :],
            )
            inner_grad = raw * column
            held_both[rows, first : first + hidden] = (
                inner_grad * up * sigmoid * (1.0 + gate * (1.0 - sigmoid))
            ).astype(BF16)
            held_both[rows, first + hidden : first + 2 * hidden] = (inner_grad * active).astype(BF16)

        def sums(add):
            for part in range(SLOTS):
                cols = slice(4 * block * part, 4 * block * (part + 1))
                w_both = weights[chunk, part, :, :, :both].reshape(4 * block, both)
                w_down = weights[chunk, part, :, :, both:].reshape(4 * block, hidden * CHUNK)
                mix = dot(held_down[rows, :], w_down, NT)
                dx = dot(held_both[rows, :], w_both, NT)
                if add:
                    mix = mix + mix_sum[rows, cols].astype(F32)
                    dx = dx + dx_sum[rows, cols].astype(F32)
                mix_sum[rows, cols] = mix.astype(BF16)
                dx_sum[rows, cols] = dx.astype(BF16)

        @pl.when(chunk == 0)
        def _():
            sums(False)

        @pl.when(chunk > 0)
        def _():
            sums(True)

    @pl.when(turn >= row_steps)
    def _():
        part = turn - row_steps
        grads[chunk, part, :, :, :both] = (
            dot(xt_ref[...], held_both[...]).astype(BF16).reshape(2, 2 * block, both)
        )
        grads[chunk, part, :, :, both:] = (
            (dot(ogt_ref[...], held_down[...]) * RESIDUAL_SCALE)
            .astype(BF16)
            .reshape(2, 2 * block, hidden * CHUNK)
        )

    begin = last * steps
    for i in range(2):
        for c in range(2):
            mine = pl.ds(tokens + (2 * c + i) * EXPERT_ROWS, EXPERT_ROWS)
            there = pl.ds((2 * c + i) * EXPERT_ROWS, EXPERT_ROWS)

            @pl.when((step == begin + 2 * c + i) & (core != c))
            def _():
                for name, total, got in (("t", dx_sum, twin_rows), ("mt", mix_sum, twin_mix)):
                    copies.remote(
                        lambda: (total.at[mine], got.at[i]), (name, i), (name, i), near.twin,
                        last=False,
                    )

            @pl.when((step == begin + 2 + 2 * c + i) & (core == c))
            def _():
                for name, total, got in (("t", dx_sum, twin_rows), ("mt", mix_sum, twin_mix)):
                    copies.arrived(got.at[i], (name, i), near.twin)
                    for here in few_rows(EXPERT_ROWS):
                        at = pl.ds(mine.start + here.start, 16)
                        total[at, :] = (
                            total[at, :].astype(F32) + got[i, here, :].astype(F32)
                        ).astype(BF16)
                copies.remote(
                    lambda: (dx_sum.at[mine], dx_other.at[there]), ("o", i), ("o", i), near.over_x,
                    last=False,
                )

            @pl.when((step == begin + steps - 2 + i) & (core == c))
            def _():
                copies.arrived(dx_other.at[there], ("o", i), near.over_x)
                copies.remote(
                    lambda: (dx_other.at[there],) * 2, ("o2", i), ("o2", i), near.twin, last=False
                )

    for i in range(tiles):

        @pl.when(step == begin + tiles + i)
        def _():
            own = pl.ds(i * EXPERT_ROWS, EXPERT_ROWS)
            copies.copy(lambda own=own: (dx_sum.at[own], dx_own.at[own]), ("own", i))
            copies.remote(
                lambda own=own: (dx_sum.at[own], dx_twin.at[own]), ("own", i), ("own", i), near.twin
            )

    shares = gate_kept.shape[0]

    @pl.when(step == begin + row_steps)
    def _():
        copies.copy(lambda: (mix_sum, mix_out), "mix")
        turned = gates[...].T[:shares, :]
        gate_kept[...] = turned
        copies.remote(
            lambda: (gate_kept.at[:, pl.ds(tokens, tokens)], gate_got), ("g",), ("g",), near.over_x
        )

    @pl.when(step == begin + steps - 2)
    def _():
        copies.arrived(gate_got, ("g",), near.over_x)
        gate_full[pl.ds(pl.multiple_of(x * shares, shares), shares), :] = gate_kept[:, :tokens]
        gate_full[pl.ds(pl.multiple_of((1 - x) * shares, shares), shares), :] = gate_got[...]
        copies.remote(lambda: (gate_full, gate_twin), ("g2",), ("g2",), near.twin)

    for c in range(chunks):

        @pl.when(step == (c + 1) * steps - 1)
        def _():
            if c < SENT:
                copies.remote(
                    lambda c=c: (grads.at[c, :, 1 - y], arrived.at[c]),
                    ("sum", c), ("sum", c), near.over_y,
                )
            else:
                for k in range(SLOTS):
                    copies.copy(
                        lambda c=c, k=k: (grads.at[c, spots[k], y], near_outs[c - SENT].at[k]),
                        ("near out", c, k),
                    )
                    if c < last and k == 0:
                        copies.copy(lambda c=c: (grads.at[c, z, 1 - y], first_out), "first out")
                    elif c < last:
                        copies.remote(
                            lambda c=c, k=k: (grads.at[c, spots[k], 1 - y], late_out.at[k - 1]),
                            ("late", k), ("late", k), near.over_y,
                        )
                    else:
                        copies.copy(
                            lambda c=c, k=k: (grads.at[c, spots[k], 1 - y], far_out.at[k]),
                            ("far out", k),
                        )

    @pl.when(step == chunks * steps - 1)
    def _():
        copies.arrived(gate_twin, ("g2",), near.twin)
        gate_out[...] = gate_full[...] + gate_twin[...]
        for i in range(tiles):
            copies.arrived(
                dx_twin.at[pl.ds(i * EXPERT_ROWS, EXPERT_ROWS)], ("own", i), near.twin
            )
        for i in range(2):
            for c in range(2):
                mine = pl.ds(tokens + (2 * c + i) * EXPERT_ROWS, EXPERT_ROWS)
                there = pl.ds((2 * c + i) * EXPERT_ROWS, EXPERT_ROWS)

                @pl.when(core != c)
                def _():
                    copies.sent(lambda: (dx_sum.at[mine], twin_rows.at[i]), ("t", i), near.twin)
                    copies.sent(lambda: (mix_sum.at[mine], twin_mix.at[i]), ("mt", i), near.twin)
                    copies.arrived(dx_other.at[there], ("o2", i), near.twin)

                @pl.when(core == c)
                def _():
                    copies.sent(
                        lambda: (dx_sum.at[mine], dx_other.at[there]), ("o", i), near.over_x
                    )
                    copies.sent(lambda: (dx_other.at[there],) * 2, ("o2", i), near.twin)

        for c in range(SENT):
            for k in range(1, SLOTS):
                copies.arrived(part_outs[c].at[k - 1], ("part", c, k), near.along[k])
        for k in range(1, SLOTS):
            copies.arrived(late_out.at[k - 1], ("late", k), near.over_y)
        copies.finish()


def experts_pass(x, og, xt, ogt, combine, pairs, near, far):
    tokens, width = x.shape
    chunks, pair, columns = pairs.shape
    hidden = columns // (3 * CHUNK)
    shares = chunks * CHUNK
    row_steps = tokens // EXPERT_ROWS
    steps = row_steps + SLOTS
    inner = lax.axis_size("dp") // 16
    row_at = lambda s: ((jnp.minimum(s % steps, row_steps - 1) + row_steps // 2) % row_steps, 0)
    width_at = lambda s: (jnp.maximum(s % steps - row_steps, 0), 0)
    row = pl.BlockSpec((EXPERT_ROWS, width), row_at)
    turned = pl.BlockSpec((width // SLOTS, tokens), width_at)
    anywhere = pl.BlockSpec(memory_space=pl.ANY)
    left = chunks - SENT
    dma = pltpu.SemaphoreType.DMA
    shape = jax.ShapeDtypeStruct
    outs = pl.pallas_call(
        functools.partial(experts_kernel, inner, chunks, row_steps),
        grid=(chunks * steps,),
        in_specs=[row, row, turned, turned, pl.BlockSpec((EXPERT_ROWS, combine.shape[1]), row_at)]
        + [anywhere] * 3,
        out_specs=[anywhere] * 4
        + [pl.BlockSpec((2 * shares, tokens // 2), lambda s: (0, 0))]
        + [anywhere] * (2 * SENT + left + 3),
        out_shape=[shape((tokens // 2, width), BF16)] * 3
        + [shape((tokens, width), BF16), shape((2 * shares, tokens // 2), F32)]
        + [shape((pair, columns), BF16)] * SENT
        + [shape((SLOTS - 1, pair, columns), BF16)] * SENT
        + [shape((SLOTS, pair, columns), BF16)] * left
        + [shape((SLOTS - 1, pair, columns), BF16), shape((pair, columns), BF16)]
        + [shape((SLOTS, pair, columns), BF16)],
        scratch_shapes=[
            pltpu.VMEM((chunks + 1, SLOTS, 2, pair, columns), BF16),
            pltpu.VMEM((SENT, SLOTS, pair, columns), BF16),
            pltpu.VMEM((tokens, 2 * hidden * CHUNK), BF16),
            pltpu.VMEM((tokens, hidden * CHUNK), BF16),
            pltpu.VMEM((tokens, width), BF16),
            pltpu.VMEM((tokens, width), BF16),
            pltpu.VMEM((2, EXPERT_ROWS, width), BF16),
            pltpu.VMEM((2, EXPERT_ROWS, width), BF16),
            pltpu.VMEM((tokens, LANES), F32),
            pltpu.VMEM((shares, tokens), F32),
            pltpu.VMEM((shares, tokens // 2), F32),
            pltpu.VMEM((2 * shares, tokens // 2), F32),
            pltpu.VMEM((2 * shares, tokens // 2), F32),
            dma((48,)), dma((48,)), dma((48,)),
        ],
        compiler_params=pltpu.CompilerParams(
            vmem_limit_bytes=EXPERT_VMEM, collective_id=0, has_side_effects=True
        ),
        cost_estimate=pl.CostEstimate(
            flops=8 * tokens * width * chunks * columns,
            bytes_accessed=2 * chunks * width * columns, transcendentals=0,
        ),
        name="experts_pass",
    )(x, og, xt, ogt, combine, pairs, near, far)
    dx, mix, gate = outs[:3], outs[3], outs[4]
    rest = outs[5:]
    keep, parts, rest = rest[:SENT], rest[SENT : 2 * SENT], rest[2 * SENT :]
    return dx, mix, gate, keep, parts, rest[:left], rest[left:]


class Copies:
    def __init__(self, send, recv, local):
        self.send, self.recv, self.local = send, recv, local
        self.sends, self.recvs, self.locals, self.started = {}, {}, {}, []

    def remote(self, ends, name, arrives, device, last=True):
        sent = self.sends.setdefault(name, len(self.sends))
        got = self.recvs.setdefault(arrives, len(self.recvs))

        def make():
            source, target = ends()
            return pltpu.make_async_remote_copy(
                source, target, self.send.at[sent], self.recv.at[got],
                device_id=device, device_id_type=MESH_ID,
            )

        make().start()
        if last:
            self.started.append(lambda: make().wait_send())

    def sent(self, ends, name, device):
        source, target = ends()
        pltpu.make_async_remote_copy(
            source, target, self.send.at[self.sends[name]], self.recv.at[0],
            device_id=device, device_id_type=MESH_ID,
        ).wait_send()

    def arrived(self, place, name, device):
        got = self.recvs.setdefault(name, len(self.recvs))
        pltpu.make_async_remote_copy(
            place, place, self.send.at[0], self.recv.at[got],
            device_id=device, device_id_type=MESH_ID,
        ).wait_recv()

    def copy(self, ends, name, wait_last=True):
        at = self.locals.setdefault(name, len(self.locals))

        def make():
            return pltpu.make_async_copy(*ends(), self.local.at[at])

        make().start()
        if wait_last:
            self.started.append(lambda: make().wait())
        return lambda: make().wait()

    def wait_copy(self, ends, name):
        pltpu.make_async_copy(*ends(), self.local.at[self.locals[name]]).wait()

    def finish(self):
        for wait in self.started:
            wait()


class Neighbours:
    def __init__(self, inner):
        me = lax.axis_index("dp")
        at = me // inner
        self.core = lax.axis_index("tensor")
        self.z, self.y, self.x = at // 4, at // 2 % 2, at % 2
        self.spots = [(self.z + dz + 4) % 4 for dz in Z_FROM]
        self.along = [{"dp": me + (spot - self.z) * 4 * inner} for spot in self.spots]
        self.over_y = {"dp": me + (1 - 2 * self.y) * 2 * inner}
        self.over_x = {"dp": me + (1 - 2 * self.x) * inner}
        self.twin = {"tensor": 1 - self.core}
        self.blocks = {
            (k, other_y, other_x): self.spots[k] * 4
            + (1 - self.y if other_y else self.y) * 2
            + (1 - self.x if other_x else self.x)
            for k in range(SLOTS)
            for other_y in (0, 1)
            for other_x in (0, 1)
        }

    def greet(self):
        barrier = pltpu.get_barrier_semaphore()
        devices = [*self.along[1:], self.over_y, self.over_x, self.twin]
        for device in devices:
            pl.semaphore_signal(barrier, inc=1, device_id=device, device_id_type=MESH_ID)
        pl.semaphore_wait(barrier, len(devices))

    def block(self, k, other_y, other_x):
        return self.blocks[k, other_y, other_x]


BACK = (0, 2, 1, 3)


class Gather:
    def __init__(self, copies, near, shard, full, tag):
        self.copies, self.near, self.shard, self.full, self.tag = copies, near, shard, full, tag
        self.split = full.shape[2] // (2 * LANES) * LANES

    def source(self, k):
        return self.shard if k == 0 else self.full.at[self.near.block(k, 0, 0)]

    def begin(self):
        for k in range(1, SLOTS):
            self.copies.remote(
                lambda: (self.shard, self.full.at[self.near.block(0, 0, 0)]),
                (self.tag, "z", k), (self.tag, "z", BACK[k]), self.near.along[k],
            )
        self.full[self.near.block(0, 0, 0)] = self.shard[...]

    def spread(self, k):
        near, place = self.near, self.full.at[self.near.block(k, 0, 0)]
        if k > 0:
            self.copies.arrived(place, (self.tag, "z", k), near.along[k])
        for way, device in (("y", near.over_y), ("x", near.over_x)):
            name = (self.tag, way, k)
            self.copies.remote(
                lambda: (self.source(k), self.full.at[near.block(k, 0, 0)]), name, name, device
            )

    def cross(self, k):
        near = self.near
        from_y = self.full.at[near.block(k, 1, 0)]
        from_x = self.full.at[near.block(k, 0, 1)]
        self.copies.arrived(from_y, (self.tag, "y", k), near.over_y)
        self.copies.remote(
            lambda: (self.full.at[near.block(k, 1, 0), :, : self.split],) * 2,
            (self.tag, "one", k), (self.tag, "one", k), near.over_x,
        )
        self.copies.arrived(from_x, (self.tag, "x", k), near.over_x)
        self.copies.remote(
            lambda: (self.full.at[near.block(k, 0, 1), :, self.split :],) * 2,
            (self.tag, "two", k), (self.tag, "two", k), near.over_y,
        )

    def end(self):
        near = self.near
        for k in range(SLOTS):
            place = self.full.at[near.block(k, 1, 1)]
            self.copies.arrived(place.at[:, : self.split], (self.tag, "one", k), near.over_x)
            self.copies.arrived(place.at[:, self.split :], (self.tag, "two", k), near.over_y)


def roll_left(slab, lanes):
    return pltpu.roll(slab, LANES - lanes, 1)


def forward_kernel(
    inner, w_query, w_keyval, w_out, w_router, gains, frequency, seg_row, routes,
    gateup_hbm, down_hbm, hidden_hbm, og_hbm,
    q_full, o_full, small, normed, q_ref, k_ref, v_ref, attended, lse_ref, combine, combine_pair,
    cos, sin, seg_col, middle_hbm, x_hbm, xt_hbm, og_pair, ogt_hbm, pairs_hbm, near_hbm, far_hbm,
    hidden, gateup, down, given, pairs, bias, k_low, k_high, v_low, v_high, part, part_got, x_own, x_got,
    middle, stage, turned, columns_out, columns_got, q_shard, o_shard, send, recv, local,
):
    near = Neighbours(inner)
    copies = Copies(send, recv, local)
    tokens, width = hidden.shape
    block = width // 16
    chunks = pairs.shape[0]
    hid = down.shape[2]
    q_width = q_ref.shape[1]
    kv_slabs = k_ref.shape[1] // LANES
    slabs = q_width // LANES
    qkv_width = q_width + 2 * k_ref.shape[1]
    experts = down.shape[0]
    each = 2 + experts
    half = tokens // 2
    tiles = tokens // ROWS
    x, core = near.x, near.core
    own_half = pl.ds(pl.multiple_of(core * half, half), half)
    mine = pl.ds(pl.multiple_of(tokens + core * half, half), half)
    theirs = pl.ds(pl.multiple_of(tokens + (1 - core) * half, half), half)

    weights_in = [
        copies.copy(lambda: (gateup_hbm, gateup), "gateup", False),
        copies.copy(lambda: (down_hbm, down), "down", False),
    ]
    hidden_in = copies.copy(lambda: (hidden_hbm, hidden), "hidden", False)
    kv_width = k_ref.shape[1]
    q_shard[:, :q_width] = w_query[...].astype(BF16)
    q_shard[:, q_width : q_width + kv_width] = w_keyval[0].astype(BF16)
    q_shard[:, q_width + kv_width : qkv_width] = w_keyval[1].astype(BF16)
    o_shard[...] = w_out[...].astype(BF16)
    cos[:block, :] = jnp.zeros((block, LANES), F32)
    cos[:block, :experts] = w_router[...]
    value = jnp.concatenate([gains[...], jnp.zeros((LANES - 2, block), F32)]).T
    value = value + pltpu.roll(cos[:block, :], 2, 1)
    high = value.astype(BF16).astype(F32)
    mid = (value - high).astype(BF16).astype(F32)
    low = value - high - mid
    value = high + pltpu.roll(mid, each, 1) + pltpu.roll(low, 2 * each, 1)
    q_shard[:, qkv_width:] = value.astype(BF16)
    near.greet()
    gather_q = Gather(copies, near, q_shard, q_full, "q")
    gather_o = Gather(copies, near, o_shard, o_full, "o")
    gather_q.begin()
    gather_q.spread(0)
    copies.copy(lambda: (og_hbm, og_pair.at[pl.ds(0, tokens)]), "og")
    segment = seg_row[...].astype(F32)
    seg_col[...] = jnp.broadcast_to(segment, (8, tokens)).T[:, :1]

    def pack(c, mine):
        first = 2 * (chunks * (x if mine else 1 - x) + c)
        rows = pl.ds(pl.multiple_of(x * block, block), block)
        for e in range(CHUNK):
            for part_at in range(2):
                at = hid * (2 * e + part_at)
                value = gateup[first + e, part_at].astype(BF16)
                if mine:
                    pairs[c, rows, at : at + hid] = value
                else:
                    given[c, :, at : at + hid] = value
            at = hid * (2 * CHUNK + e)
            value = down[first + e].astype(BF16)
            if mine:
                pairs[c, rows, at : at + hid] = value
            else:
                given[c, :, at : at + hid] = value

    def swap(c):
        rows = pl.ds(pl.multiple_of(x * block, block), block)
        copies.remote(
            lambda: (given.at[c], pairs.at[c, rows]), ("s", c), ("s", c), near.over_x
        )

    def swapped(c):
        rows = pl.ds(pl.multiple_of((1 - x) * block, block), block)
        copies.arrived(pairs.at[c, rows], ("s", c), near.over_x)

    def ring_one(c):
        copies.remote(
            lambda: (pairs.at[c], near_hbm.at[c, 0]), ("up", c), ("r", c, 1), near.along[2]
        )
        copies.remote(
            lambda: (pairs.at[c], near_hbm.at[c, 1]), ("down", c), ("r", c, 2), near.along[1]
        )

    def ring_two(c):
        copies.arrived(near_hbm.at[c, 0], ("r", c, 1), near.along[1])
        copies.remote(
            lambda: (near_hbm.at[c, 0], near_hbm.at[c, 2]), ("two", c), ("r", c, 3), near.along[2]
        )

    def over_y(c, k):
        copies.remote(
            lambda: (pairs.at[c] if k == 0 else near_hbm.at[c, k - 1], far_hbm.at[c, k]),
            ("f", c, k), ("f", c, k), near.over_y,
        )

    def ring_got(c, k):
        copies.arrived(near_hbm.at[c, k - 1], ("r", c, k), near.along[k])

    def turn_tile(source, target, name, side):
        copies.copy(lambda: (source, stage.at[side]), (name, "in"), False)()
        turned[side] = stage[side].T
        return copies.copy(lambda: (turned.at[side], target), (name, "out"), False)

    waits = [None, None]

    def turn_next(source, target, name, side):
        if waits[side] is not None:
            waits[side]()
        waits[side] = turn_tile(source, target, name, side)

    for wait in weights_in:
        wait()
    pack(0, False)
    swap(0)
    pack(0, True)
    gather_q.spread(1)
    gather_q.spread(2)
    pack(1, False)
    pack(1, True)
    gather_q.cross(0)
    gather_q.spread(3)
    half_width = HEAD_DIM // 2
    lane = lax.broadcasted_iota(jnp.int32, (ROWS, LANES), 1)
    for at in range(0, tokens, ROWS):
        rows = slice(at, at + ROWS)
        earlier = jnp.where(segment < seg_col[rows, :], 1.0, 0.0)
        position = (at + lax.broadcasted_iota(jnp.int32, (ROWS, 1), 0)).astype(F32)
        position = position - jnp.sum(earlier, axis=1, keepdims=True)
        angle = position * frequency[...]
        cos[rows, :] = jnp.cos(angle)
        wave = jnp.sin(angle)
        sin[rows, :] = jnp.where(lane % HEAD_DIM < half_width, -wave, wave)
    gather_q.cross(1)
    gather_q.cross(2)
    gather_q.cross(3)
    gather_o.begin()
    gather_o.spread(0)
    swap(1)
    pack(2, False)
    pack(2, True)
    pack(3, False)
    pack(3, True)
    fill_bias(bias, seg_col, segment)
    for tile in range(tiles):
        rows = pl.ds(tile * ROWS, ROWS)
        turn_next(og_hbm.at[rows], ogt_hbm.at[:, rows], ("og", tile), tile % 2)
    hidden_in()
    gather_q.end()
    pieces = q_full[:, :, qkv_width:].reshape(width, LANES)
    wide = pieces.astype(F32)
    summed = wide + roll_left(wide, each) + roll_left(wide, 2 * each)
    small[...] = summed.T[: small.shape[0], :]
    swapped(0)
    ring_one(0)
    over_y(0, 0)
    swap(2)
    swap(3)

    def project(tile, carry):
        rows = pl.ds(pl.multiple_of(tile * ROWS, ROWS), ROWS)
        for here in few_rows(ROWS):
            value = hidden[pl.ds(pl.multiple_of(tile * ROWS + here.start, 16), 16), :].astype(F32)
            inverse = lax.rsqrt(jnp.mean(value * value, axis=1, keepdims=True) + NORM_EPSILON)
            stage[0, here, :] = (value * inverse * small[0:1, :]).astype(BF16)
        low = stage[0]
        normed[:, rows] = low.T
        cosine, sine = cos[rows, :], sin[rows, :]
        for g in range(slabs + 2 * kv_slabs):
            lanes = slice(g * LANES, (g + 1) * LANES)
            if g % 2 == 0:
                two = slice(g * LANES, (g + 2) * LANES)
                lin_two = dot(low, q_full[:, :, two].reshape(width, 2 * LANES))
            lin = lin_two[:, (g % 2) * LANES : (g % 2 + 1) * LANES]
            if g < slabs + kv_slabs:
                lin = lin * cosine + rotate_halves(lin) * sine
            if g < slabs:
                q_ref[rows, lanes] = lin.astype(BF16)
            elif g < slabs + kv_slabs:
                at = (g - slabs) * LANES
                k_ref[rows, at : at + LANES] = lin.astype(BF16)
            else:
                at = (g - slabs - kv_slabs) * LANES
                v_ref[rows, at : at + LANES] = lin.astype(BF16)

        @pl.when(tile == 1)
        def _():
            gather_o.spread(1)

        @pl.when(tile == 2)
        def _():
            gather_o.spread(2)
            gather_o.cross(0)

        return carry

    lax.fori_loop(0, tiles, project, 0)
    for j in range(kv_slabs):
        lanes = slice(j * LANES, (j + 1) * LANES)
        spread_heads(k_ref[:, lanes], k_low, k_high, 2 * j)
        spread_heads(v_ref[:, lanes], v_low, v_high, 2 * j)

    def attend(g, carry):
        lanes = pl.ds(pl.multiple_of(g * LANES, LANES), LANES)
        kv_even, kv_odd = (2 * g) // 3, (2 * g + 1) // 3
        for at in range(0, tokens, ROWS):
            rows = slice(at, at + ROWS)
            upto = at + ROWS
            queries = q_ref[rows, lanes]
            total = None
            stats = []
            for keys, values, kv_at in ((k_low, v_low, kv_even), (k_high, v_high, kv_odd)):
                scores = dot(queries, keys[kv_at, :upto, :], NT) * SCORE_SCALE + bias[rows, :upto]
                highest = jnp.max(scores, axis=1, keepdims=True)
                weights = jnp.exp(scores - highest)
                whole = jnp.sum(weights, axis=1, keepdims=True)
                probability = (weights * (1.0 / whole)).astype(BF16)
                one = dot(probability, values[kv_at, :upto, :])
                total = one if total is None else total + one
                stats.append(highest + jnp.log(whole))
            attended[rows, lanes] = total.astype(BF16)
            across = jnp.where(half_mask(ROWS, False), stats[0], stats[1]).T
            lse_ref[g, 0:1, rows] = across[0:1, :]
            lse_ref[g, 1:2, rows] = across[HEAD_DIM : HEAD_DIM + 1, :]

        @pl.when(g == 0)
        def _():
            gather_o.spread(3)
            gather_o.cross(1)
            gather_o.cross(2)

        @pl.when(g == 1)
        def _():
            ring_two(0)
            over_y(0, 1)
            ring_got(0, 2)
            over_y(0, 2)
            swapped(1)
            ring_one(1)
            over_y(1, 0)
            copies.remote(
                lambda: (og_hbm.at[own_half], og_pair.at[mine]), ("og",), ("og",), near.over_x
            )

        @pl.when(g == 2)
        def _():
            gather_o.cross(3)

        @pl.when(g == 4)
        def _():
            gather_o.end()

        @pl.when(g == slabs - 1)
        def _():
            ring_got(0, 3)
            over_y(0, 3)
            swapped(2)
            ring_one(2)
            over_y(2, 0)

        return carry

    lax.fori_loop(0, slabs, attend, 0)

    def project_out(step, carry):
        tile = (step + 2 * (1 - core)) % tiles
        rows = pl.ds(pl.multiple_of(tile * ROWS, ROWS), ROWS)
        low = attended[rows, :]
        for group in range(SLOTS):
            cols = slice(4 * block * group, 4 * block * (group + 1))
            weight = o_full[4 * group : 4 * (group + 1)].reshape(4 * block, q_width)
            part[rows, cols] = dot(low, weight, NT).astype(BF16)
        return carry

    for step in range(tiles):
        project_out(step, 0)
        tile = (step + 2 * (1 - core)) % tiles
        rows = pl.ds(pl.multiple_of(tile * ROWS, ROWS), ROWS)
        copies.remote(
            lambda rows=rows: (part.at[rows], part_got.at[rows]),
            ("p", step), ("p", step), near.twin,
        )
    router = q_full[:, :, qkv_width:].reshape(width, LANES)
    for step in range(tiles):
        tile = (step + 2 * core) % tiles
        rows = pl.ds(pl.multiple_of(tile * ROWS, ROWS), ROWS)
        copies.arrived(part_got.at[rows], ("p", step), near.twin)
        side = step % 2
        if step >= 2:
            middle_out[side]()
        elif step == 0:
            middle_out = [None, None]
        for here in few_rows(ROWS):
            at = pl.ds(pl.multiple_of(tile * ROWS + here.start, 16), 16)
            total = hidden[at, :].astype(F32) + RESIDUAL_SCALE * (
                part[at, :].astype(F32) + part_got[at, :].astype(F32)
            )
            middle[side, here, :] = total
            inverse = lax.rsqrt(jnp.mean(total * total, axis=1, keepdims=True) + NORM_EPSILON)
            value = total * inverse * small[1:2, :]
            high = value.astype(BF16)
            x_own[at, :] = high
            rest = value - high.astype(F32)
            mid = rest.astype(BF16)
            stage[0, here, :] = mid
            stage[1, here, :] = (rest - mid.astype(F32)).astype(BF16)
        middle_out[side] = copies.copy(
            lambda rows=rows, side=side: (middle.at[side], middle_hbm.at[rows]), ("m", step), False
        )
        copies.copy(lambda rows=rows: (x_own.at[rows], x_hbm.at[rows]), ("x", step))
        if step < 2:
            copies.remote(
                lambda rows=rows: (x_own.at[rows], x_got.at[rows]),
                ("x", step), ("x", step), near.over_x,
            )
        one, two, three = dot(x_own[rows, :], router), dot(stage[0], router), dot(stage[1], router)
        logits = one + roll_left(one, each) + roll_left(one, 2 * each) + two + roll_left(two, each)
        logits = roll_left(logits + three, 2)
        lane = lax.broadcasted_iota(jnp.int32, (ROWS, LANES), 1)
        chosen = lane < 0
        route = routes[:, rows].astype(F32).T
        for k in range(routes.shape[0]):
            chosen = chosen | (route[:, k : k + 1] == lane.astype(F32))
        logits = jnp.where(chosen, logits, MASK_VALUE)
        powers = jnp.exp(logits - jnp.max(logits, axis=1, keepdims=True))
        powers = jnp.where(chosen, powers, 0.0)
        combine[rows, :] = powers * (1.0 / jnp.sum(powers, axis=1, keepdims=True))
        if step == 0:
            swapped(3)
            copies.copy(lambda: (pairs, pairs_hbm), "pairs")
        if step == 1:
            ring_two(1)
            over_y(1, 1)
            ring_got(1, 2)
            over_y(1, 2)

    shares = experts // 2
    flipped = combine[...].T
    kept = jnp.where(x == 0, flipped[:shares, :], flipped[shares : 2 * shares, :])
    gone = jnp.where(x == 0, flipped[shares : 2 * shares, :], flipped[:shares, :])
    columns_out[...] = gone
    copies.remote(lambda: (columns_out, columns_got), ("c",), ("c",), near.over_x)
    combine_pair[:tokens, :] = kept.T
    ring_two(2)
    ring_got(1, 3)
    over_y(1, 3)

    copies.arrived(og_pair.at[mine], ("og",), near.over_x)
    copies.remote(lambda: (og_pair.at[mine],) * 2, ("og2",), ("og2",), near.twin)
    for tile in range(tiles):
        rows = pl.ds(tile * ROWS, ROWS)
        if waits[tile % 2] is not None:
            waits[tile % 2]()
        turned[tile % 2] = x_own[rows, :].T
        waits[tile % 2] = copies.copy(
            lambda rows=rows, side=tile % 2: (turned.at[side], xt_hbm.at[:, rows]),
            ("xt", tile), False,
        )
    copies.arrived(columns_got, ("c",), near.over_x)
    combine_pair[tokens:, :] = columns_got[...].T
    copies.arrived(og_pair.at[theirs], ("og2",), near.twin)
    order = [(step + 2 * core) % tiles for step in range(2)]
    order += [(step + 2 * (1 - core)) % tiles for step in range(2)]

    def og_rows(step):
        return pl.ds(pl.multiple_of(tokens + order[step] * ROWS, ROWS), ROWS)

    def og_load(step):
        return copies.copy(
            lambda: (og_pair.at[og_rows(step)], stage.at[step % 2]), ("ogin", step), False
        )

    loaded = og_load(0)
    for step in range(tiles):
        loaded()
        if step + 1 < tiles:
            loaded = og_load(step + 1)
        side = step % 2
        waits[side]()
        turned[side] = stage[side].T
        waits[side] = copies.copy(
            lambda step=step, side=side: (turned.at[side], ogt_hbm.at[:, og_rows(step)]),
            ("ogt", step), False,
        )
    for step in range(tiles):
        rows = pl.ds(pl.multiple_of(order[step] * ROWS, ROWS), ROWS)
        there = pl.ds(pl.multiple_of(tokens + order[step] * ROWS, ROWS), ROWS)
        if step < 2:
            copies.arrived(x_got.at[rows], ("x", step), near.over_x)
            copies.remote(
                lambda rows=rows: (x_got.at[rows],) * 2, ("x2", step), ("x2", step), near.twin
            )
        else:
            copies.arrived(x_got.at[rows], ("x2", step - 2), near.twin)
        copies.copy(
            lambda rows=rows, there=there: (x_got.at[rows], x_hbm.at[there]), ("xg", step)
        )
        side = step % 2
        waits[side]()
        turned[side] = x_got[rows, :].T
        waits[side] = copies.copy(
            lambda there=there, side=side: (turned.at[side], xt_hbm.at[:, there]),
            ("xgt", step), False,
        )
    for wait in waits + middle_out:
        wait()
    ring_got(2, 2)
    ring_got(2, 3)
    for c in range(LATE + 1):
        for k in range(SLOTS if c < LATE else 1):
            copies.arrived(far_hbm.at[c, k], ("f", c, k), near.over_y)
    copies.finish()


def forward_pass(weights, frequency, segments, routes, gateup, down, hidden, og):
    tokens, width = hidden.shape
    experts, hid = down.shape[0], down.shape[2]
    block, q_width = weights[0].shape
    kv_width = weights[1].shape[2]
    q_columns = q_width + 2 * kv_width + LANES
    slabs, kv_heads = q_width // LANES, kv_width // HEAD_DIM
    chunks = experts // (2 * CHUNK)
    columns = 3 * CHUNK * hid
    anywhere, vmem = pl.BlockSpec(memory_space=pl.ANY), vmem_spec()
    shape = jax.ShapeDtypeStruct
    inner = lax.axis_size("dp") // 16
    dma = pltpu.SemaphoreType.DMA
    return pl.pallas_call(
        functools.partial(forward_kernel, inner),
        in_specs=[vmem] * 8 + [anywhere] * 4,
        out_specs=[vmem] * 14 + [anywhere] * 8,
        out_shape=[
            shape((16, block, q_columns), BF16),
            shape((16, block, q_width), BF16),
            shape((24, width), F32),
            shape((width, tokens), BF16),
            shape((tokens, q_width), BF16),
            shape((tokens, kv_width), BF16),
            shape((tokens, kv_width), BF16),
            shape((tokens, q_width), BF16),
            shape((slabs, 8, tokens), F32),
            shape((tokens, LANES), F32),
            shape((2 * tokens, experts // 2), F32),
            shape((tokens, LANES), F32),
            shape((tokens, LANES), F32),
            shape((tokens, 1), F32),
            shape((tokens, width), F32),
            shape((2 * tokens, width), BF16),
            shape((width, 2 * tokens), BF16),
            shape((2 * tokens, width), BF16),
            shape((width, 2 * tokens), BF16),
            shape((chunks, 2 * block, columns), BF16),
            shape((chunks - 1, SLOTS - 1, 2 * block, columns), BF16),
            shape((LATE + 1, SLOTS, 2 * block, columns), BF16),
        ],
        scratch_shapes=[
            pltpu.VMEM((tokens, width), BF16),
            pltpu.VMEM(gateup.shape, gateup.dtype),
            pltpu.VMEM(down.shape, down.dtype),
            pltpu.VMEM((chunks, block, columns), BF16),
            pltpu.VMEM((chunks, 2 * block, columns), BF16),
            pltpu.VMEM((tokens, tokens), F32),
        ]
        + [pltpu.VMEM((kv_heads, tokens, LANES), BF16)] * 4
        + [pltpu.VMEM((tokens, width), BF16)] * 4
        + [
            pltpu.VMEM((2, ROWS, width), F32),
            pltpu.VMEM((2, ROWS, width), BF16),
            pltpu.VMEM((2, width, ROWS), BF16),
            pltpu.VMEM((experts // 2, tokens), F32),
            pltpu.VMEM((experts // 2, tokens), F32),
            pltpu.VMEM((block, q_columns), BF16),
            pltpu.VMEM((block, q_width), BF16),
            dma((80,)), dma((80,)), dma((60,)),
        ],
        compiler_params=pltpu.CompilerParams(
            vmem_limit_bytes=EXPERT_VMEM, collective_id=1, has_side_effects=True
        ),
        name="forward_pass",
    )(*weights, frequency, segments[None, :], routes.T, gateup, down, hidden, og)


class Scatter:
    def __init__(self, copies, near, grad, one, two, got_y, got_x, got_z, share, tag):
        self.copies, self.near, self.grad, self.share, self.tag = copies, near, grad, share, tag
        self.one, self.two, self.got_y, self.got_x, self.got_z = one, two, got_y, got_x, got_z
        self.split = one.shape[2]

    def begin(self, k):
        near = self.near
        self.copies.remote(
            lambda: (self.grad.at[near.block(k, 1, 1), :, : self.split], self.one.at[k]),
            (self.tag, "one", k), (self.tag, "one", k), near.over_x,
        )
        self.copies.remote(
            lambda: (self.grad.at[near.block(k, 1, 1), :, self.split :], self.two.at[k]),
            (self.tag, "two", k), (self.tag, "two", k), near.over_y,
        )

    def cross(self, k):
        near, grad, split = self.near, self.grad, self.split
        self.copies.arrived(self.one.at[k], (self.tag, "one", k), near.over_x)
        at = near.block(k, 1, 0)
        for here in few_rows(grad.shape[1]):
            grad[at, here, :split] = (
                grad[at, here, :split].astype(F32) + self.one[k, here, :].astype(F32)
            ).astype(BF16)
        self.copies.remote(
            lambda: (grad.at[near.block(k, 1, 0)], self.got_y.at[k]),
            (self.tag, "y", k), (self.tag, "y", k), near.over_y,
        )
        self.copies.arrived(self.two.at[k], (self.tag, "two", k), near.over_y)
        at = near.block(k, 0, 1)
        for here in few_rows(grad.shape[1]):
            grad[at, here, split:] = (
                grad[at, here, split:].astype(F32) + self.two[k, here, :].astype(F32)
            ).astype(BF16)
        self.copies.remote(
            lambda: (grad.at[near.block(k, 0, 1)], self.got_x.at[k]),
            (self.tag, "x", k), (self.tag, "x", k), near.over_x,
        )

    def plane(self, k):
        near, grad = self.near, self.grad
        self.copies.arrived(self.got_y.at[k], (self.tag, "y", k), near.over_y)
        self.copies.arrived(self.got_x.at[k], (self.tag, "x", k), near.over_x)
        at = near.block(k, 0, 0)
        for here in few_rows(grad.shape[1]):
            total = grad[at, here, :].astype(F32) + self.got_y[k, here, :].astype(F32)
            total = total + self.got_x[k, here, :].astype(F32)
            if k == 0:
                self.share[here, :] = total
            else:
                grad[at, here, :] = total.astype(BF16)
        if k == 0:
            return
        self.copies.remote(
            lambda: (grad.at[near.block(k, 0, 0)], self.got_z.at[BACK[k] - 1]),
            (self.tag, "z", k), (self.tag, "z", BACK[k]), near.along[k],
        )

    def end(self):
        for k in range(1, SLOTS):
            self.copies.arrived(self.got_z.at[k - 1], (self.tag, "z", k), self.near.along[k])
            for here in few_rows(self.share.shape[0]):
                self.share[here, :] = self.share[here, :] + self.got_z[k - 1, here, :].astype(F32)


STRIP = 128


def backward_kernel(
    inner,
    o_full, q_ref, k_ref, v_ref, attended, lse_ref, cos, sin, seg_col, seg_row, small, combine,
    gate_turned, q_hbm, normed_hbm, hidden_hbm, og_hbm, middle_hbm, dx_own, dx_twin, dx_other,
    mix_pair, *refs,
):
    keeps, refs = refs[:SENT], refs[SENT:]
    parts, refs = refs[:SENT], refs[SENT:]
    near_two, near_three, late_got, far_first, far_three = refs[:5]
    q_share, o_share, input_grad, block_out, kept_out, given_got, mid_grad = refs[5:12]
    far_got, first_got, z_two, z_three, mix_twin, mix_other = refs[12:18]
    (
        attended_grad, lin_grad, o_grad, q_grad, o_one, o_two, o_y, o_x, o_z,
        q_one, q_two, q_y, q_x, q_z, part_got, pieces, z_send, z_keep, given, kept,
        strips, wide_in, wide_out, strip_out, router_rows, gate_columns, small_sum,
        send, recv, local, strip_sem, wide_sem, out_sem,
    ) = refs[18:]
    near = Neighbours(inner)
    copies = Copies(send, recv, local)
    tokens, width = hidden_hbm.shape
    block = width // 16
    x, core = near.x, near.core
    half = tokens // 2
    q_width = q_ref.shape[1]
    kv_width = k_ref.shape[1]
    kv_slabs, slabs = kv_width // LANES, q_width // LANES
    qkv_width = q_width + 2 * kv_width
    experts = gate_turned.shape[0]
    each = 2 + experts
    strip_count = tokens // STRIP
    ours = pl.ds(0, tokens)
    half_mine = pl.ds(pl.multiple_of(tokens + core * half, half), half)
    there = pl.ds(pl.multiple_of(core * half, half), half)
    not_there = pl.ds(pl.multiple_of((1 - core) * half, half), half)
    scatter_o = Scatter(copies, near, o_grad, o_one, o_two, o_y, o_x, o_z, o_share, "o")
    scatter_q = Scatter(copies, near, q_grad, q_one, q_two, q_y, q_x, q_z, q_share, "q")
    z_gots = [*parts, z_two, z_three]

    def y_ends(c, k):
        if c == SENT:
            return near_two.at[k], first_got if k == 0 else late_got.at[k - 1]
        return near_three.at[k], far_got.at[k]

    def y_load(c, k, i, which):
        if 0 in which:
            copies.copy(lambda: (y_ends(c, k)[0], pieces.at[2 * i]), ("own", c, k), False)
        if 1 in which:
            copies.copy(lambda: (y_ends(c, k)[1], pieces.at[2 * i + 1]), ("got", c, k), False)

    def y_sum(c, k, i):
        copies.wait_copy(lambda: (y_ends(c, k)[0], pieces.at[2 * i]), ("own", c, k))
        copies.wait_copy(lambda: (y_ends(c, k)[1], pieces.at[2 * i + 1]), ("got", c, k))
        if k > 0 and c > SENT:
            copies.sent(
                lambda: (z_send.at[k - 1], z_two.at[BACK[k] - 1]), (SENT, "z", k), near.along[k]
            )
        target = z_keep.at[c - SENT] if k == 0 else z_send.at[k - 1]
        for here in few_rows(target.shape[0]):
            target[here, :] = (
                pieces[2 * i, here, :].astype(F32) + pieces[2 * i + 1, here, :].astype(F32)
            ).astype(BF16)
        if k == 0:
            return
        copies.remote(
            lambda: (z_send.at[k - 1], z_gots[c].at[BACK[k] - 1]),
            (c, "z", k), (c, "z", BACK[k]), near.along[k], last=c > SENT,
        )

    def far_arrived(k):
        copies.arrived(far_got.at[k], ("far", k), near.over_y)

    def chunk_ends(c, k):
        return keeps[c] if k == 0 else z_gots[c].at[k - 1], pieces.at[k]

    def load_chunk(c):
        for k in range(1 if c >= SENT else 0, SLOTS):
            if c >= SENT:
                copies.arrived(z_gots[c].at[k - 1], (c, "z", k), near.along[k])
            copies.copy(lambda k=k: chunk_ends(c, k), (c, "sum", k), False)

    def sum_chunk(c):
        for k in range(1 if c >= SENT else 0, SLOTS):
            copies.wait_copy(lambda: chunk_ends(c, k), (c, "sum", k))
        if c >= 2:
            copies.wait_copy(lambda: (kept.at[c % 2], kept_out.at[c - 2]), ("kept", c - 2))
        for base, mine in ((x * block, True), ((1 - x) * block, False)):
            for here, rows in zip(few_rows(block), few_rows(block, base)):
                total = (pieces[0, rows, :] if c < SENT else z_keep[c - SENT, rows, :]).astype(F32)
                for k in range(1, SLOTS):
                    total = total + pieces[k, rows, :].astype(F32)
                if mine:
                    kept[c % 2, here, :] = total
                else:
                    given[c, here, :] = total.astype(BF16)
        copies.copy(lambda: (kept.at[c % 2], kept_out.at[c]), ("kept", c), c >= 2)
        copies.remote(
            lambda: (given.at[c], given_got.at[c]), ("given", c), ("given", c), near.over_x
        )

    def strip_rows(t):
        return pl.ds(pl.multiple_of(t * STRIP, STRIP), STRIP)

    def strip_loads(t, sources, wide):
        side = t % 2
        rows = strip_rows(t)
        loads = [
            pltpu.make_async_copy(source.at[rows], strips.at[i, side], strip_sem.at[i, side])
            for i, source in enumerate(sources)
        ]
        if wide is not None:
            loads.append(
                pltpu.make_async_copy(wide.at[rows], wide_in.at[side], wide_sem.at[side])
            )
        return loads

    def strip_store(t, source, target):
        side = t % 2
        return pltpu.make_async_copy(
            source.at[side], target.at[strip_rows(t)], out_sem.at[side]
        )

    def over_strips(sources, wide, source, target, compute):
        for load in strip_loads(0, sources, wide):
            load.start()

        def one(t, carry):
            side = t % 2

            @pl.when(t + 1 < strip_count)
            def _():
                for load in strip_loads(t + 1, sources, wide):
                    load.start()

            for load in strip_loads(t, sources, wide):
                load.wait()

            @pl.when(t >= 2)
            def _():
                strip_store(t - 2, source, target).wait()

            compute(t, side)
            strip_store(t, source, target).start()
            return carry

        lax.fori_loop(0, strip_count, one, 0)
        for t in (strip_count - 2, strip_count - 1):
            strip_store(t, source, target).wait()

    for i, k in enumerate((1, 2)):
        y_load(SENT, k, i, (0, 1))
    near.greet()
    for k in (1, 2, 3, 0):
        copies.remote(
            lambda k=k: (far_three.at[k], far_got.at[k]), ("far", k), ("far", k), near.over_y
        )
    copies.remote(lambda: (far_first, first_got), ("first",), ("first",), near.over_y)
    copies.remote(
        lambda: (mix_pair.at[half_mine], mix_other.at[there]), ("mo",), ("mo",), near.over_x
    )
    copies.remote(lambda: (mix_pair.at[ours], mix_twin), ("mt",), ("mt",), near.twin)
    y_sum(SENT, 1, 0)
    y_load(SENT, 3, 0, (0, 1))
    y_sum(SENT, 2, 1)
    y_sum(SENT, 3, 0)
    load_chunk(0)

    router = small[2 : 2 + experts, :]
    high = router.astype(BF16).astype(F32)
    mid = (router - high).astype(BF16).astype(F32)
    low = router - high - mid
    router_rows[...] = jnp.concatenate(
        [high, mid, low, high, mid, high, jnp.zeros((LANES - 6 * experts, width), F32)]
    ).astype(BF16)
    gate_columns[...] = jnp.concatenate(
        [gate_turned[...], jnp.zeros((LANES - experts, tokens), F32)]
    ).T
    small_sum[...] = jnp.zeros_like(small_sum)

    def middle_part(turned_back):
        def compute(t, side):
            rows = strip_rows(t)
            gates, grads = combine[rows, :], gate_columns[rows, :]
            logit = gates * (grads - jnp.sum(gates * grads, axis=1, keepdims=True))
            one = logit.astype(BF16).astype(F32)
            two = (logit - one).astype(BF16).astype(F32)
            three = (logit - one - two).astype(BF16).astype(F32)

            def moved(piece, by):
                return pltpu.roll(piece, by * experts, 1)

            row = one + moved(one, 1) + moved(one, 2) + moved(two, 3) + moved(two, 4)
            row = (row + moved(three, 5)).astype(BF16)
            wide_out[side] = dot(row, router_rows[...])
            gain = small[1:2, :]
            gain_part = None
            back, n_one, n_two, n_three = (
                strip_out.at[0], strip_out.at[1], z_keep.at[0], z_keep.at[1]
            )
            for here in few_rows(STRIP):
                upstream = strips[0, side, here, :].astype(F32) + strips[1, side, here, :].astype(F32)
                upstream = upstream + strips[2, side, here, :].astype(F32)
                upstream = upstream + wide_out[side, here, :]
                middle = wide_in[side, here, :]
                inverse = lax.rsqrt(jnp.mean(middle * middle, axis=1, keepdims=True) + NORM_EPSILON)
                scaled = middle * inverse
                weighted = upstream * gain
                mean_term = jnp.mean(weighted * scaled, axis=1, keepdims=True)
                grad = strips[3, side, here, :].astype(F32) + inverse * (
                    weighted - scaled * mean_term
                )
                wide_out[side, here, :] = grad
                back[here, :] = (RESIDUAL_SCALE * grad).astype(BF16)
                gained = jnp.sum(upstream * scaled, axis=0, keepdims=True)
                gain_part = gained if gain_part is None else gain_part + gained
                normed = scaled * gain
                piece = normed.astype(BF16)
                n_one[here, :] = piece
                rest = normed - piece.astype(F32)
                piece = rest.astype(BF16)
                n_two[here, :] = piece
                n_three[here, :] = (rest - piece.astype(F32)).astype(BF16)
            small_sum[0:1, :] += gain_part
            strip = pl.ds(0, STRIP)
            turned_back[:, rows] = back[...].T
            attended_grad[rows, :] = dot(back[...], o_full[...].reshape(width, q_width)).astype(BF16)
            columns = (one + moved(two, 1) + moved(three, 2)).T[: 3 * experts, :].astype(BF16)
            a, b, c = (
                dot(columns, n_one[...]), dot(columns, n_two[strip, :]), dot(columns, n_three[strip, :])
            )
            e = experts
            small_sum[8 : 8 + e, :] += (
                a[:e] + a[e : 2 * e] + a[2 * e :] + b[:e] + b[e : 2 * e] + c[:e]
            )

        over_strips([dx_own, dx_twin, dx_other, og_hbm], middle_hbm, wide_out, mid_grad, compute)
        for group in range(SLOTS):
            rows = slice(4 * block * group, 4 * block * (group + 1))
            o_grad[4 * group : 4 * (group + 1)] = (
                dot(turned_back[rows, :], attended[...]).astype(BF16).reshape(4, block, q_width)
            )

    pl.run_scoped(middle_part, pltpu.VMEM((width, tokens), BF16))
    for k in (1, 2, 3, 0):
        scatter_o.begin(k)

    def attention_part(bias0, bias1, bias2, bias3, k_low, k_high, v_low, v_high, dk, dv, dq):
        biases = (bias0, bias1, bias2, bias3)
        for at, bias in enumerate(biases):
            upto = bias.shape[0]
            keys_at = lax.broadcasted_iota(jnp.int32, bias.shape, 0)
            rows_at = at * ROWS + lax.broadcasted_iota(jnp.int32, bias.shape, 1)
            same = seg_col[:upto, :] == seg_row[:, at * ROWS : (at + 1) * ROWS].astype(F32)
            bias[...] = jnp.where((rows_at >= keys_at) & same, 0.0, MASK_VALUE).astype(F32)
        for j in range(kv_slabs):
            lanes = slice(j * LANES, (j + 1) * LANES)
            spread_heads(k_ref[:, lanes], k_low, k_high, 2 * j)
            spread_heads(v_ref[:, lanes], v_low, v_high, 2 * j)
        dk[...] = jnp.zeros_like(dk)
        dv[...] = jnp.zeros_like(dv)

        def slab(g, carry):
            lanes = pl.ds(pl.multiple_of(g * LANES, LANES), LANES)
            kv_even, kv_odd = (2 * g) // 3, (2 * g + 1) // 3
            for at, bias in enumerate(biases):
                rows = slice(at * ROWS, (at + 1) * ROWS)
                upto = (at + 1) * ROWS
                queries, grads = q_ref[rows, lanes], attended_grad[rows, lanes]
                turned = (grads.astype(F32) * attended[rows, lanes].astype(F32)).T
                zero = jnp.zeros_like(queries)
                dq_part = None
                for upper, keys, values, kv_at in (
                    (False, k_low, v_low, kv_even), (True, k_high, v_high, kv_odd)
                ):
                    first = HEAD_DIM if upper else 0
                    delta = jnp.sum(turned[first : first + HEAD_DIM, :], axis=0, keepdims=True)
                    head = 1 if upper else 0
                    total = lse_ref[g, head : head + 1, rows]
                    keys_here = keys[kv_at, :upto, :]
                    scores = dot(keys_here, queries, NT) * SCORE_SCALE + bias[...]
                    probability = jnp.exp(scores - total)
                    prob_grad = dot(values[kv_at, :upto, :], grads, NT)
                    score_grad = (probability * (prob_grad - delta)).astype(BF16)
                    mask = half_mask(ROWS, upper)
                    dv[kv_at, :upto, :] += dot(
                        probability.astype(BF16), jnp.where(mask, grads, zero)
                    )
                    dk[kv_at, :upto, :] += dot(score_grad, jnp.where(mask, queries, zero))
                    one = dot(score_grad, keys_here, TN)
                    dq_part = one if dq_part is None else dq_part + one
                dq[rows, :] = dq_part * SCORE_SCALE
            whole = dq[...]
            lin_grad[:, lanes] = (
                whole * cos[...] - rotate_halves(whole) * sin[...]
            ).astype(BF16)

            @pl.when(g == 1)
            def _():
                for k in (1, 2, 3, 0):
                    scatter_o.cross(k)

            @pl.when(g == 2)
            def _():
                sum_chunk(0)
                y_load(SENT + 1, 1, 0, (0,))
                y_load(SENT + 1, 2, 1, (0,))

            @pl.when(g == 3)
            def _():
                far_arrived(1)
                y_load(SENT + 1, 1, 0, (1,))
                far_arrived(2)
                y_load(SENT + 1, 2, 1, (1,))
                far_arrived(3)
                y_sum(SENT + 1, 1, 0)
                y_load(SENT + 1, 3, 0, (0, 1))
                y_sum(SENT + 1, 2, 1)
                y_sum(SENT + 1, 3, 0)
                load_chunk(1)

            @pl.when(g == 4)
            def _():
                for k in (1, 2, 3, 0):
                    scatter_o.plane(k)
                sum_chunk(1)
                far_arrived(0)
                y_load(SENT + 1, 0, 0, (0, 1))
                copies.arrived(first_got, ("first",), near.over_y)
                y_load(SENT, 0, 1, (0, 1))

            return carry

        lax.fori_loop(0, slabs, slab, 0)
        low = half_mask(tokens, False)

        def joined(sums, j):
            one, two = sums[2 * j], sums[2 * j + 1]
            one = one + pltpu.roll(one, HEAD_DIM, 1)
            two = two + pltpu.roll(two, HEAD_DIM, 1)
            return jnp.where(low, one, two)

        for j in range(kv_slabs):
            at = q_width + j * LANES
            whole = joined(dk, j) * SCORE_SCALE
            lin_grad[:, at : at + LANES] = (
                whole * cos[...] - rotate_halves(whole) * sin[...]
            ).astype(BF16)
            at = at + kv_width
            lin_grad[:, at : at + LANES] = joined(dv, j).astype(BF16)

    kv_shape = (2 * kv_slabs, tokens, LANES)
    pl.run_scoped(
        attention_part,
        *[pltpu.VMEM(((at + 1) * ROWS, ROWS), F32) for at in range(tokens // ROWS)],
        *[pltpu.VMEM(kv_shape, BF16)] * 4,
        *[pltpu.VMEM(kv_shape, F32)] * 2,
        pltpu.VMEM((tokens, LANES), F32),
    )

    def last_part(normed_turned, q_full, part):
        normed_in = copies.copy(lambda: (normed_hbm, normed_turned), "normed", False)
        weights_in = copies.copy(lambda: (q_hbm, q_full), "q weights", False)
        columns = jnp.concatenate(
            [
                small_sum[0:1, :], small_sum[8 : 8 + experts, :],
                jnp.zeros((LANES - 1 - experts, width), F32),
            ]
        ).T
        q_grad[:, :, qkv_width:] = columns.astype(BF16).reshape(16, block, LANES)
        normed_in()
        for k in (1, 2, 3, 0):
            spot = near.spots[k]
            rows = pl.ds(pl.multiple_of(spot * 4 * block, 4 * block), 4 * block)
            q_grad[pl.ds(spot * 4, 4), :, :qkv_width] = (
                dot(normed_turned[rows, :], lin_grad[...])
                .astype(BF16)
                .reshape(4, block, qkv_width)
            )
            scatter_q.begin(k)
        weights_in()

        def project(tile):
            rows = pl.ds(tile * ROWS, ROWS)
            for group in range(SLOTS):
                cols = slice(4 * block * group, 4 * block * (group + 1))
                weight = q_full[4 * group : 4 * (group + 1), :, :qkv_width]
                part[rows, cols] = dot(
                    lin_grad[rows, :], weight.reshape(4 * block, qkv_width), NT
                ).astype(BF16)
            copies.remote(
                lambda: (part.at[rows], part_got.at[rows]), ("n", tile), ("n", tile), near.twin,
                last=False,
            )

        project(0)
        project(1)
        for k in (1, 2, 3, 0):
            scatter_q.cross(k)
        y_sum(SENT + 1, 0, 0)
        y_sum(SENT, 0, 1)
        load_chunk(2)
        project(2)
        project(3)
        scatter_o.end()
        copies.arrived(mix_other.at[there], ("mo",), near.over_x)
        copies.remote(lambda: (mix_other.at[there],) * 2, ("m2",), ("m2",), near.twin)
        sum_chunk(2)
        for tile in range(tokens // ROWS):
            rows = pl.ds(tile * ROWS, ROWS)
            copies.arrived(part_got.at[rows], ("n", tile), near.twin)

        def finish_rows(t, side):
            for here in few_rows(STRIP):
                at = pl.ds(pl.multiple_of(t * STRIP + here.start, 16), 16)
                value = strips[0, side, here, :].astype(F32)
                inverse = lax.rsqrt(jnp.mean(value * value, axis=1, keepdims=True) + NORM_EPSILON)
                upstream = part[at, :].astype(F32) + part_got[at, :].astype(F32)
                scaled = value * inverse
                weighted = upstream * small[0:1, :]
                mean_term = jnp.mean(weighted * scaled, axis=1, keepdims=True)
                wide_out[side, here, :] = wide_in[side, here, :] + inverse * (
                    weighted - scaled * mean_term
                )

        over_strips([hidden_hbm], mid_grad, wide_out, input_grad, finish_rows)
        for k in (1, 2, 3, 0):
            scatter_q.plane(k)
        load_chunk(3)
        for tile in range(tokens // ROWS):
            rows = pl.ds(tile * ROWS, ROWS)
            copies.sent(lambda: (part.at[rows], part_got.at[rows]), ("n", tile), near.twin)

    pl.run_scoped(
        last_part,
        pltpu.VMEM((width, tokens), BF16), pltpu.VMEM(q_hbm.shape, BF16),
        pltpu.VMEM((tokens, width), BF16),
    )
    sum_chunk(3)
    copies.arrived(mix_twin, ("mt",), near.twin)
    copies.arrived(mix_other.at[not_there], ("m2",), near.twin)

    def mix_rows(t, side):
        for here in few_rows(STRIP):
            mix = strips[0, side, here, :].astype(F32) + strips[1, side, here, :].astype(F32)
            mix = mix + strips[2, side, here, :].astype(F32)
            strip_out[side, here, :] = (wide_in[side, here, :] + RESIDUAL_SCALE * mix).astype(BF16)

    over_strips([mix_pair, mix_twin, mix_other], middle_hbm, strip_out, block_out, mix_rows)
    scatter_q.end()
    for c in range(2 * SENT):
        copies.arrived(given_got.at[c], ("given", c), near.over_x)
    copies.finish()


def backward_pass(
    o_full, q, k, v, attended, lse, cosine, sine, seg_col, segments, small, combine, gate_turned,
    q_full, normed, hidden, og, middle, dx, mix, keep, parts, near_grads, far_grads,
):
    tokens, width = hidden.shape
    q_width, kv_width = q.shape[1], k.shape[1]
    block, q_columns = q_full.shape[1:]
    qkv_width = q_width + 2 * kv_width
    pair, columns = keep[0].shape
    chunks = 2 * SENT
    experts = gate_turned.shape[0]
    anywhere, vmem = pl.BlockSpec(memory_space=pl.ANY), vmem_spec()
    shape = jax.ShapeDtypeStruct
    dma = pltpu.SemaphoreType.DMA
    inner = lax.axis_size("dp") // 16

    def scatter_scratch(total):
        split = total // (2 * LANES) * LANES
        return [
            pltpu.VMEM((SLOTS, block, split), BF16),
            pltpu.VMEM((SLOTS, block, total - split), BF16),
            pltpu.VMEM((SLOTS, block, total), BF16),
            pltpu.VMEM((SLOTS, block, total), BF16),
            pltpu.VMEM((SLOTS - 1, block, total), BF16),
        ]

    values = (
        o_full, q, k, v, attended, lse, cosine, sine, seg_col, segments[None, :],
        small, combine, gate_turned,
    )
    far_values = (
        q_full, normed, hidden, og, middle, *dx, mix, *keep, *parts, *near_grads, *far_grads,
    )
    return pl.pallas_call(
        functools.partial(backward_kernel, inner),
        in_specs=[vmem] * len(values) + [anywhere] * len(far_values),
        out_specs=[vmem] * 2 + [anywhere] * 11,
        out_shape=[
            shape((block, q_columns), F32),
            shape((block, q_width), F32),
            shape((tokens, width), F32),
            shape((tokens, width), BF16),
            shape((chunks, block, columns), F32),
            shape((chunks, block, columns), BF16),
            shape((tokens, width), F32),
            shape((SLOTS, pair, columns), BF16),
            shape((pair, columns), BF16),
            shape((SLOTS - 1, pair, columns), BF16),
            shape((SLOTS - 1, pair, columns), BF16),
            shape((tokens, width), BF16),
            shape((tokens, width), BF16),
        ],
        scratch_shapes=[
            pltpu.VMEM((tokens, q_width), BF16),
            pltpu.VMEM((tokens, qkv_width), BF16),
            pltpu.VMEM((16, block, q_width), BF16),
            pltpu.VMEM((16, block, q_columns), BF16),
        ]
        + scatter_scratch(q_width)
        + scatter_scratch(q_columns)
        + [
            pltpu.VMEM((tokens, width), BF16),
            pltpu.VMEM((SLOTS, pair, columns), BF16),
            pltpu.VMEM((SLOTS - 1, pair, columns), BF16),
            pltpu.VMEM((2, pair, columns), BF16),
            pltpu.VMEM((chunks, block, columns), BF16),
            pltpu.VMEM((2, block, columns), F32),
            pltpu.VMEM((4, 2, STRIP, width), BF16),
            pltpu.VMEM((2, STRIP, width), F32),
            pltpu.VMEM((2, STRIP, width), F32),
            pltpu.VMEM((2, STRIP, width), BF16),
            pltpu.VMEM((LANES, width), BF16),
            pltpu.VMEM((tokens, LANES), F32),
            pltpu.VMEM((8 + experts, width), F32),
            dma((80,)), dma((80,)), dma((60,)), dma((4, 2)), dma((2,)), dma((2,)),
        ],
        compiler_params=pltpu.CompilerParams(
            vmem_limit_bytes=EXPERT_VMEM, collective_id=2, has_side_effects=True
        ),
        name="backward_pass",
    )(*values, *far_values)


def whole_call(kernel, values, outs, earlier=(), name=None):
    return pl.pallas_call(
        with_earlier(kernel, len(values), len(earlier)),
        in_specs=[vmem_spec()] * len(values) + any_specs(earlier),
        out_specs=[vmem_spec()] * len(outs),
        out_shape=[jax.ShapeDtypeStruct(shape, dtype) for shape, dtype in outs],
        compiler_params=pltpu.CompilerParams(vmem_limit_bytes=VMEM_BYTES),
        name=name,
    )(*values, *earlier)


def fence_kernel(*refs):
    count = len(refs) // 2
    for value, out in zip(refs[:count], refs[count:]):
        out[...] = value[...]


def fence_all(values, *earlier):
    return whole_call(fence_kernel, values, [(v.shape, v.dtype) for v in values], earlier, "fence")


def fence(value, *earlier):
    return fence_all([value], *earlier)[0]


def sum_y_kernel(near, got, *outs):
    for k, out in enumerate(outs):
        out[...] = (near[k].astype(F32) + got[k].astype(F32)).astype(BF16)


def sum_y(near, got, *earlier):
    outs = [(near.shape[1:], BF16)] * SLOTS
    return whole_call(sum_y_kernel, [near, got], outs, earlier, "sum_y")


def sum_z_kernel(x_at, *refs):
    kept, given = refs[-2:]
    half = kept.shape[1]
    for c in range(kept.shape[0]):
        parts = refs[SLOTS * c : SLOTS * (c + 1)]
        for rows, out in ((x_at[0], kept), (1 - x_at[0], given)):
            rows = pl.ds(pl.multiple_of(rows * half, half), half)
            total = parts[0][rows, :].astype(F32)
            for part in parts[1:]:
                total = total + part[rows, :].astype(F32)
            out[c] = total.astype(out.dtype)


def sum_z(x_at, chunks, *earlier):
    count = len(chunks)
    pair, columns = chunks[0][0].shape
    flat = [part for parts in chunks for part in parts]
    return pl.pallas_call(
        with_earlier(sum_z_kernel, 1 + len(flat), len(earlier)),
        in_specs=[smem_spec()] + [vmem_spec()] * len(flat) + any_specs(earlier),
        out_specs=[vmem_spec()] * 2,
        out_shape=[
            jax.ShapeDtypeStruct((count, pair // 2, columns), F32),
            jax.ShapeDtypeStruct((count, pair // 2, columns), BF16),
        ],
        compiler_params=pltpu.CompilerParams(vmem_limit_bytes=VMEM_BYTES),
        name="sum_z",
    )(x_at, *flat, *earlier)


def sum_parts_kernel(parts, out):
    total = parts[0].astype(F32)
    for c in range(1, parts.shape[0]):
        total = total + parts[c].astype(F32)
    out[...] = total.astype(BF16)


def sum_parts(parts, *earlier):
    chunks, tokens, width = parts.shape
    return pl.pallas_call(
        with_earlier(sum_parts_kernel, 1, len(earlier)),
        grid=(tokens // EXPERT_ROWS,),
        in_specs=[pl.BlockSpec((chunks, EXPERT_ROWS, width), lambda s: (0, s, 0))]
        + any_specs(earlier),
        out_specs=pl.BlockSpec((EXPERT_ROWS, width), lambda s: (s, 0)),
        out_shape=jax.ShapeDtypeStruct((tokens, width), BF16),
        compiler_params=pltpu.CompilerParams(vmem_limit_bytes=VMEM_BYTES),
        name="sum_parts",
    )(parts, *earlier)


def adam_attention_kernel(q_share, o_share, *refs):
    states, outs = refs[:9], refs[9:18]
    gain_part = refs[18]
    q_width, kv_width = states[0].shape[1], states[3].shape[2]
    rate = (MODEL_DIM // 12) ** (-0.5)
    grad = q_share[:, :q_width]
    total = jnp.sum(states[0][...].astype(BF16).astype(F32) * grad, axis=1, keepdims=True)
    results = [
        adam_update(states[0][...], grad, states[1][...], states[2][...], rate, WEIGHT_DECAY)
    ]
    for out, result in zip(outs[:3], results[0]):
        out[...] = result
    for c in range(2):
        first = q_width + c * kv_width
        grad = q_share[:, first : first + kv_width]
        value = states[3][c]
        total = total + jnp.sum(value.astype(BF16).astype(F32) * grad, axis=1, keepdims=True)
        results = adam_update(value, grad, states[4][c], states[5][c], rate, WEIGHT_DECAY)
        for out, result in zip(outs[3:6], results):
            out[c] = result
    gain_part[...] = total
    results = adam_update(
        states[6][...], o_share[...], states[7][...], states[8][...],
        max(1, QUERY_HEADS * HEAD_DIM // 96) ** (-0.5), WEIGHT_DECAY,
    )
    for out, result in zip(outs[6:], results):
        out[...] = result


def adam_attention(q_share, o_share, states):
    outs = [(one.shape, F32) for one in states] + [((q_share.shape[0], 1), F32)]
    return whole_call(adam_attention_kernel, [q_share, o_share, *states], outs, (), "adam_attention")


def adam_experts_kernel(x_at, kept, got, *refs):
    states, outs = refs[:6], refs[6:]
    own = kept.shape[1]
    hidden = states[0].shape[3]
    mine = pl.program_id(0) // (pl.num_programs(0) // 2) == x_at[0]
    grad = jnp.where(mine, kept[0], got[0].astype(F32))
    for e in range(CHUNK):
        for part in range(2):
            first = hidden * (2 * e + part)
            results = adam_update(
                states[0][e, part], grad[:, first : first + hidden],
                states[1][e, part], states[2][e, part], MODEL_DIM ** (-0.5), WEIGHT_DECAY,
            )
            for out, result in zip(outs[:3], results):
                out[e, part] = result
        first = hidden * (2 * CHUNK + e)
        results = adam_update(
            states[3][e], grad[:, first : first + hidden], states[4][e], states[5][e],
            max(1, F // 256) ** (-0.5), WEIGHT_DECAY,
        )
        for out, result in zip(outs[3:], results):
            out[e] = result


def adam_experts(x_at, kept, got, gateup, down):
    chunks, own, columns = kept.shape
    experts, hidden = down[0].shape[0], down[0].shape[2]
    share = pl.BlockSpec((1, own, columns), lambda j: (j % chunks, 0, 0))
    big = pl.BlockSpec((CHUNK, 2, own, hidden), lambda j: (j, 0, 0, 0))
    small = pl.BlockSpec((CHUNK, own, hidden), lambda j: (j, 0, 0))
    return pl.pallas_call(
        adam_experts_kernel,
        grid=(experts // CHUNK,),
        in_specs=[smem_spec(), share, share] + [big] * 3 + [small] * 3,
        out_specs=[big] * 3 + [small] * 3,
        out_shape=[jax.ShapeDtypeStruct(gateup[0].shape, F32)] * 3
        + [jax.ShapeDtypeStruct(down[0].shape, F32)] * 3,
        compiler_params=pltpu.CompilerParams(vmem_limit_bytes=VMEM_BYTES),
        name="adam_experts",
    )(x_at, kept, got, *gateup, *down)


def join_tokens_kernel(own, first, second, out, turned):
    half = own.shape[0] // 2
    for at, part in ((0, own[:half, :]), (half, own[half:, :]), (2 * half, first[...]), (3 * half, second[...])):
        out[at : at + half, :] = part
        turned[:, at : at + half] = part.T


def join_tokens(own, first, second, *earlier):
    tokens, width = own.shape
    return pl.pallas_call(
        with_earlier(join_tokens_kernel, 3, len(earlier)),
        in_specs=[vmem_spec()] * 3 + any_specs(earlier),
        out_specs=[vmem_spec()] * 2,
        out_shape=[
            jax.ShapeDtypeStruct((2 * tokens, width), own.dtype),
            jax.ShapeDtypeStruct((width, 2 * tokens), own.dtype),
        ],
        compiler_params=pltpu.CompilerParams(vmem_limit_bytes=VMEM_BYTES),
        name="join_tokens",
    )(own, first, second, *earlier)


def move(array, dz=0, dy=0, dx=0):
    total = lax.axis_size("dp")
    inner = total // 16
    pairs = []
    for at in range(16):
        z, y, x = at // 4, at // 2 % 2, at % 2
        to = ((z + dz) % 4) * 4 + (y ^ dy) * 2 + (x ^ dx)
        pairs += [(at * inner + i, to * inner + i) for i in range(inner)]
    return lax.ppermute(array, "dp", pairs)


def place():
    at = lax.axis_index("dp") // (lax.axis_size("dp") // 16)
    return at // 4, at // 2 % 2, at % 2


def inner_groups(total):
    inner = total // 16
    return [[at * inner + i for i in range(inner)] for at in range(16)]


def inner_gather(shard, axis):
    total = lax.axis_size("dp")
    if total == 16:
        return shard
    return lax.all_gather(
        shard, "dp", axis=axis, tiled=True, axis_index_groups=inner_groups(total)
    )


def inner_scatter(share, axis):
    total = lax.axis_size("dp")
    if total == 16:
        return share
    return lax.psum_scatter(
        share, "dp", scatter_dimension=axis, tiled=True, axis_index_groups=inner_groups(total)
    )


def block_rows(parts, rows):
    z, y, x = place()
    starts = []
    for dz, dy, dx in parts:
        starts.append((((z + dz + 4) % 4) * 4 + (y ^ dy) * 2 + (x ^ dx)) * rows)
    return jnp.stack(starts).astype(jnp.int32)


def gather_z(shard):
    return jnp.stack([shard] + [move(shard, dz=-dz) for dz in Z_FROM[1:]])


def gather_ring(shard):
    below, above = move(shard, dz=1), move(shard, dz=-1)
    return [shard, below, above, move(below, dz=1)]


def send_z(parts):
    return [move(parts[k].astype(BF16), dz=Z_FROM[k]) for k in range(1, SLOTS)]


def scatter_z(parts, moved=None):
    result = parts[0]
    for one in moved or send_z(parts):
        result = result + one.astype(F32)
    return result


def gather_plane(own):
    half = own.shape[-1] // 2
    along_y, along_x = move(own, dy=1), move(own, dx=1)
    both = (move(along_y[..., :half], dx=1), move(along_x[..., half:], dy=1))
    return own, along_y, along_x, *both


def scatter_plane(pieces):
    own, along_y, along_x, both_one, both_two = pieces
    half = both_one.shape[-1]
    got_one, got_two = move(both_one, dx=1), move(both_two, dy=1)
    pass_y = jnp.concatenate(
        [(along_y[..., :half].astype(F32) + got_one.astype(F32)).astype(BF16), along_y[..., half:]],
        axis=-1,
    )
    pass_x = jnp.concatenate(
        [along_x[..., :half], (along_x[..., half:].astype(F32) + got_two.astype(F32)).astype(BF16)],
        axis=-1,
    )
    got_y, got_x = move(pass_y, dy=1), move(pass_x, dx=1)
    return scatter_z(
        [
            own[k].astype(F32) + got_y[k].astype(F32) + got_x[k].astype(F32)
            for k in range(SLOTS)
        ]
    )


PLANE = [(dz, dy, dx) for dy, dx in ((0, 0), (1, 0), (0, 1), (1, 1)) for dz in Z_FROM]


def join_kernel(rows_at, *refs):
    pieces, out = refs[:-1], refs[-1]
    slots, own, width = pieces[0].shape
    half = width // 2
    for at in range(4 * slots):
        rows = pl.ds(pl.multiple_of(rows_at[at], own), own)
        group, slot = at // slots, at % slots
        if group < 3:
            out[rows, :] = pieces[group][slot]
        else:
            out[rows, :half] = pieces[3][slot]
            out[rows, half:] = pieces[4][slot]


def part_kernel(rows_at, whole, *pieces):
    slots, own, width = pieces[0].shape
    half = width // 2
    for at in range(4 * slots):
        rows = pl.ds(pl.multiple_of(rows_at[at], own), own)
        group, slot = at // slots, at % slots
        if group < 3:
            pieces[group][slot] = whole[rows, :]
        else:
            pieces[3][slot] = whole[rows, :half]
            pieces[4][slot] = whole[rows, half:]


def smem_spec():
    return pl.BlockSpec(memory_space=pltpu.SMEM)


def vmem_spec():
    return pl.BlockSpec(memory_space=pltpu.VMEM)


def join_blocks(rows_at, pieces, earlier=()):
    slots, own, width = pieces[0].shape
    return pl.pallas_call(
        with_earlier(join_kernel, 6, len(earlier)),
        in_specs=[smem_spec()] + [vmem_spec()] * 5 + any_specs(earlier),
        out_specs=vmem_spec(),
        out_shape=jax.ShapeDtypeStruct((4 * slots * own, width), BF16),
        compiler_params=pltpu.CompilerParams(vmem_limit_bytes=VMEM_BYTES),
        name="join_blocks",
    )(rows_at, *pieces, *earlier)


def part_blocks(rows_at, whole, earlier=()):
    own, width = whole.shape[0] // (4 * SLOTS), whole.shape[1]
    full = jax.ShapeDtypeStruct((SLOTS, own, width), BF16)
    half = jax.ShapeDtypeStruct((SLOTS, own, width // 2), BF16)
    return pl.pallas_call(
        with_earlier(part_kernel, 2, len(earlier)),
        in_specs=[smem_spec(), vmem_spec()] + any_specs(earlier),
        out_specs=[vmem_spec()] * 5,
        out_shape=[full] * 3 + [half] * 2,
        compiler_params=pltpu.CompilerParams(vmem_limit_bytes=VMEM_BYTES),
        name="part_blocks",
    )(rows_at, whole, *earlier)


def after(value, *earlier):
    marks = []
    for one in earlier:
        slots = one.shape[0] if one.shape[0] == SLOTS else 1
        lead, rest = (slots > 1) * 1, one.ndim - 1
        marks.append(lax.slice(one, (lead,) + (0,) * rest, (slots,) + (1,) * rest))
    return lax.optimization_barrier((value, *marks))[0]


def split_three(values):
    high = values.astype(BF16)
    rest = values - high.astype(F32)
    middle = rest.astype(BF16)
    low = (rest - middle.astype(F32)).astype(BF16)
    return [high, middle, low]


def swap_cores(part):
    return lax.ppermute(part, "tensor", [(0, 1), (1, 0)])


def pair_sum(part):
    return part.astype(F32) + swap_cores(part).astype(F32)


def norm_backward(values, inverse, gain_row, upstream):
    scaled = values * inverse
    weighted = upstream * gain_row
    mean_term = jnp.mean(weighted * scaled, axis=-1, keepdims=True)
    return (inverse * (weighted - scaled * mean_term), jnp.sum(upstream * scaled, axis=0))


def adam_update(value, gradient, mean_old, square_old, rate, decay):
    mean_new = FIRST_DECAY * mean_old + (1.0 - FIRST_DECAY) * gradient
    square_new = SECOND_DECAY * square_old + (1.0 - SECOND_DECAY) * gradient * gradient
    mean_hat = mean_new / (1.0 - FIRST_DECAY**STEP)
    square_hat = square_new / (1.0 - SECOND_DECAY**STEP)
    updated = value - rate * (mean_hat / (jnp.sqrt(square_hat) + ADAM_EPSILON) + decay * value)
    return (mean_new, square_new, updated)


def shards(
    hidden_in,
    out_grad,
    routes,
    segments,
    norm_gains,
    gains_mean,
    gains_square,
    w_query,
    query_mean,
    query_square,
    key_value_weight,
    key_value_first_moment,
    key_value_second_moment,
    w_out,
    out_mean,
    out_square,
    w_router,
    router_mean,
    router_square,
    w_gateup,
    gateup_mean,
    gateup_square,
    w_down,
    down_mean,
    down_square,
):
    tokens, width = hidden_in.shape
    own = w_query.shape[0]
    experts, hidden = w_down.shape[0], w_down.shape[1]
    q_width, kv_width = w_query.shape[1], key_value_weight.shape[2]
    qkv_width = q_width + 2 * kv_width
    each = 2 + experts
    half_experts = experts // 2
    block = width // 16
    z_at, y_at, x_at = place()
    core = lax.axis_index("tensor")
    plane_rows = block_rows(PLANE, block)
    turned_down = [one.transpose(0, 2, 1) for one in (w_down, down_mean, down_square)]
    gateup_rows, down_rows = w_gateup, turned_down[0]
    if lax.axis_size("dp") > 16:
        gateup_rows = inner_gather(w_gateup.astype(BF16), 2)
        down_rows = inner_gather(down_rows.astype(BF16), 1)
    chunks = experts // (2 * CHUNK)
    first = x_at == 0
    half_width = HEAD_DIM // 2
    frequency = ROPE_BASE ** (-2.0 * jnp.arange(half_width, dtype=F32) / HEAD_DIM)
    frequency = jnp.concatenate([frequency] * 4)[None, :]
    turned_out = [one.T for one in (w_out, out_mean, out_square)]
    weights = (
        inner_gather(w_query, 0), inner_gather(key_value_weight, 1),
        inner_gather(turned_out[0], 0), inner_gather(w_router, 0), inner_gather(norm_gains, 1),
    )
    (
        qkv_blocks, out_blocks, small, normed_low, queries, keys, values, attended, lse,
        combine, combine_pair, cosine, sine, seg_col,
        middle, x_pair, x_turned, og_pair, og_turned, pairs, near, far,
    ) = forward_pass(
        weights, frequency, segments, routes, gateup_rows, down_rows, hidden_in, out_grad
    )
    dx, mix_pair, gate_turned, keep, z_got, near_grads, far_grads = experts_pass(
        x_pair, og_pair, x_turned, og_turned, combine_pair, pairs, near, far
    )
    qkv_share, output_share, input_grad, block_out, kept_share, got_share = backward_pass(
        out_blocks, queries, keys, values, attended, lse, cosine, sine, seg_col, segments, small,
        combine, gate_turned, qkv_blocks, normed_low, hidden_in, out_grad, middle, dx, mix_pair, keep,
        z_got, near_grads, far_grads,
    )[:6]
    kept_share, got_share = inner_scatter(kept_share, 1), inner_scatter(got_share, 1)
    x_here = x_at.astype(jnp.int32)[None]
    output_share = inner_scatter(output_share, 0)
    qkv_share = inner_scatter(qkv_share, 0)
    *attention_results, gain_one_part = adam_attention(
        qkv_share, output_share,
        [
            w_query, query_mean, query_square, key_value_weight, key_value_first_moment,
            key_value_second_moment, *turned_out,
        ],
    )
    gain_one_share = pair_sum(gain_one_part.T) / norm_gains[:1]
    gains_share = jnp.concatenate([gain_one_share, qkv_share[:, qkv_width][None, :]])
    router_share = qkv_share[:, qkv_width + 1 : qkv_width + 1 + experts]

    gains_result = adam_update(norm_gains, gains_share, gains_mean, gains_square, GAIN_RATE, 0.0)
    router_result = adam_update(
        w_router, router_share, router_mean, router_square, (4 * MODEL_DIM) ** (-0.5), WEIGHT_DECAY
    )
    expert_results = adam_experts(
        x_here, kept_share, got_share,
        (w_gateup, gateup_mean, gateup_square), turned_down,
    )
    expert_results = [*expert_results[:3], *(one.transpose(0, 2, 1) for one in expert_results[3:])]
    return (
        (block_out, input_grad)
        + gains_result
        + tuple(attention_results[:6])
        + tuple(one.T for one in attention_results[6:])
        + router_result
        + tuple(expert_results)
    )


def solution(mesh):
    tokens, gains = P("dp", None), P(None, "dp")
    query, keyval, out = P("dp", "tensor"), P(None, "dp", "tensor"), P("tensor", "dp")
    router, gateup, down = P("dp", None), P(None, None, "dp", "tensor"), P(None, "tensor", "dp")
    states = tuple(
        spec for one in (gains, query, keyval, out, router, gateup, down) for spec in (one,) * 3
    )
    return jax.shard_map(
        shards,
        mesh=mesh,
        in_specs=(tokens, tokens, tokens, P("dp")) + states,
        out_specs=(tokens, tokens) + states,
        check_vma=False,
    )
```

profile of v0, /device:TPU:3, one launch (start us, length us, event | category | flops | bytes accessed | tf_op | source)
XLA Modules:
  0.0 624.0 jit_solution(11874652834271751455)
XLA Ops:
  0.7 1.4 copy.70.w_router
  2.1 0.6 maximum_bitcast_fusion.frequency
  2.7 189.8 %forward_pass.1 = (bf16[16,96,1408]{2,1,0:T(8,128)(2,1)}, bf16[16,96,768]{2,1,0:T(8,128)(2,1)}, f32[24,1536]{1,0:T(8,128)}, bf16[1536,1024]{1,0:T(8,128)(2,1)}, ...) custom-call(f32[96,768]{1,0:T(8,128)} %refs_2_.2, ...), custom_call_target="tpu_custom_call" | custom-call | tf_op jit(solution)/shard_map/forward_pass/pallas_call | solution.py:1262
  192.5 205.9 %experts_pass.1 = (bf16[1024,1536]{1,0:T(8,128)(2,1)}, bf16[1024,1536]{1,0:T(8,128)(2,1)}, bf16[1024,1536]{1,0:T(8,128)(2,1)}, bf16[2048,1536]{1,0:T(8,128)(2,1)...) custom-call(bf16[2048,1536]{1,0:T(8,128)(2,1)} %get-tuple-element.92, ...), custom_call_target="tpu_custom_call" | custom-call | flops 154618822656 | bytes 18874368 | tf_op jit(solution)/shard_map/experts_pass/pallas_call | solution.py:642
  398.4 183.7 %backward_pass.1 = (f32[96,1408]{1,0:T(8,128)}, f32[96,768]{1,0:T(8,128)}, f32[1024,1536]{1,0:T(8,128)}, bf16[1024,1536]{1,0:T(8,128)(2,1)}, f32[4,96,1536]{2,1,...) custom-call(bf16[16,96,768]{2,1,0:T(8,128)(2,1)} %get-tuple-element., ...), custom_call_target="tpu_custom_call" | custom-call | tf_op jit(solution)/shard_map/backward_pass/pallas_call | solution.py:1872
  582.1 0.0 copy-start.2
  582.1 0.0 copy-start.3
  582.1 0.0 copy-start.4
  582.1 0.0 copy-start.1
  582.2 3.7 adam_attention.1
  585.9 0.9 reduce
  586.8 9.4 %collective-permute-start = (f32[1,96]{1,0:T(1,128)S(1)}, f32[1,96]{1,0:T(1,128)S(1)}, u32[]{:S(2)}, u32[]{:S(2)}) collective-permute-start(f32[1,96]{1,0:T(1,128)S(1)} %bitcast.32), channel_id=1, source_target_pairs={{0,1},{1,0},{2,3},{3,2},{4,5},{5,4},{6,7},{7,6},{8,9},{9,8},{10,11... | collective-permute-start | bytes 1160 | tf_op jit(solution)/shard_map/ppermute | solution.py:2283
  596.2 0.9 slice_reduce_fusion
  597.1 0.0 copy-done.2
  597.1 0.0 copy-done.3
  597.2 0.1 copy.72
  597.2 0.0 copy-done.4
  597.3 0.1 copy.73
  597.4 0.1 copy.74
  597.4 0.0 copy-done.1
  597.5 0.9 multiply_subtract_fusion
  598.4 0.7 copy.76
  599.0 0.7 copy.77
  599.7 0.7 copy.78
  600.4 0.0 copy-start.5
  600.4 0.0 copy-start.6
  600.4 0.0 copy-start.7
  600.4 0.0 copy-start
  600.4 15.1 %adam_experts.1 = (f32[16,2,96,256]{3,2,1,0:T(8,128)}, f32[16,2,96,256]{3,2,1,0:T(8,128)}, f32[16,2,96,256]{3,2,1,0:T(8,128)}, f32[16,96,256]{2,1,0:T(8,128)}, f...) custom-call(s32[1]{0:T(128)} %bitcast.10.x_at, f32[4,96,1536]{2,1,0:T(8,128)} %get-tuple-element.131.kept, ...), custom_call_target="tpu_custom_call" | custom-call | tf_op jit(solution)/shard_map/adam_experts/pallas_call | solution.py:2072
  615.5 0.0 collective-permute-done
  615.5 0.0 copy-done.5
  615.5 0.0 copy-done.6
  615.6 0.0 copy-done.7
  615.6 0.6 multiply_subtract_fusion.1
  616.2 0.0 copy-done
  616.2 1.7 copy.81
  617.8 5.9 copy.82
  (5 shorter events, 0.0 us)
Async XLA Ops:
  582.1 15.0 %copy-start.2 = (f32[96,16]{0,1:T(8,128)S(1)}, f32[96,16]{0,1:T(8,128)}, u32[]{:S(2)}) copy-start(f32[96,16]{0,1:T(8,128)} %param.41) | copy-start | bytes 18436
  582.1 15.0 %copy-start.3 = (f32[96,16]{0,1:T(8,128)S(1)}, f32[96,16]{0,1:T(8,128)}, u32[]{:S(2)}) copy-start(f32[96,16]{0,1:T(8,128)} %param.42) | copy-start | bytes 18436
  582.1 15.1 %copy-start.4 = (f32[96,16]{0,1:T(8,128)S(1)}, f32[96,16]{0,1:T(8,128)}, u32[]{:S(2)}) copy-start(f32[96,16]{0,1:T(8,128)} %param.43) | copy-start | bytes 18436
  582.1 15.3 %copy-start.1 = (f32[96,16]{1,0:T(8,128)S(1)}, f32[96,16]{1,0:T(8,128)}, u32[]{:S(2)}) copy-start(f32[96,16]{1,0:T(8,128)} %copy.70.w_router) | copy-start | bytes 18436
  586.8 28.7 %collective-permute-start = (f32[1,96]{1,0:T(1,128)S(1)}, f32[1,96]{1,0:T(1,128)S(1)}, u32[]{:S(2)}, u32[]{:S(2)}) collective-permute-start(f32[1,96]{1,0:T(1,128)S(1)} %bitcast.32), channel_id=1, source_target_pairs={{0,1},{1,0},{2,3},{3,2},{4,5},{5,4},{6,7},{7,6},{8,9},{9,8},{10,11... | collective-permute-start | bytes 1160 | tf_op jit(solution)/shard_map/ppermute | solution.py:2283
  600.4 15.1 %copy-start.5 = (f32[2,96]{1,0:T(2,128)S(1)}, f32[2,96]{1,0:T(2,128)}, u32[]{:S(2)}) copy-start(f32[2,96]{1,0:T(2,128)} %gains.1) | copy-start | bytes 2308
  600.4 15.2 %copy-start.6 = (f32[2,96]{1,0:T(2,128)S(1)}, f32[2,96]{1,0:T(2,128)}, u32[]{:S(2)}) copy-start(f32[2,96]{1,0:T(2,128)} %param.31) | copy-start | bytes 2308
  600.4 15.2 %copy-start.7 = (f32[2,96]{1,0:T(2,128)S(1)}, f32[2,96]{1,0:T(2,128)}, u32[]{:S(2)}) copy-start(f32[2,96]{1,0:T(2,128)} %param.30) | copy-start | bytes 2308
  600.4 15.8 %copy-start = (bf16[1024,1536]{1,0:T(8,128)(2,1)S(1)}, bf16[1024,1536]{1,0:T(8,128)(2,1)}, u32[]{:S(2)}) copy-start(bf16[1024,1536]{1,0:T(8,128)(2,1)} %get-tuple-element.237) | copy-start | bytes 9437188
where the time goes:
time: 632 us; the launch traced here: 624 us
  Pallas kernels  598 us (95%)
  local copies, waits for them, and re-layouts  12.2 us (2%)
  starting transfers between devices  9.42 us (1%)
    pallas_call x1, Pallas kernels, experts_pass(): pl.pallas_call(functools.partial(experts_kernel, inner, chunks, row_steps...  206 us
    pallas_call x1, Pallas kernels, forward_pass(): pl.pallas_call(functools.partial(forward_kernel, inner), in_specs=[vmem]...  190 us
    pallas_call x1, Pallas kernels, backward_pass(): pl.pallas_call(functools.partial(backward_kernel, inner), in_specs=[vmem]...  184 us
    pallas_call x1, Pallas kernels, adam_experts(): pl.pallas_call(adam_experts_kernel, grid=(experts // CHUNK,), in_specs=[s...  15.1 us
  transfers between devices with their start and end apart: 1, of which 0 were waited for; matrix products, arithmetic and copies ran while one was open for 1% of the time, Pallas kernels for 2%

commit v1 on v0

--- a/solution.py
+++ b/solution.py
@@ -828,10 +828,12 @@
 def forward_kernel(
     inner, w_query, w_keyval, w_out, w_router, gains, frequency, seg_row, routes,
     gateup_hbm, down_hbm, hidden_hbm, og_hbm,
-    q_full, o_full, small, normed, q_ref, k_ref, v_ref, attended, lse_ref, combine, combine_pair,
-    cos, sin, seg_col, middle_hbm, x_hbm, xt_hbm, og_pair, ogt_hbm, pairs_hbm, near_hbm, far_hbm,
+    small, combine, combine_pair, seg_col,
+    q_full_out, o_full_out, normed_out, q_out, k_out, v_out, attended_out, lse_out, cos_out, sin_out,
+    middle_hbm, x_hbm, xt_hbm, og_pair, ogt_hbm, pairs_hbm, near_hbm, far_hbm,
     hidden, gateup, down, given, pairs, bias, k_low, k_high, v_low, v_high, part, part_got, x_own, x_got,
-    middle, stage, turned, columns_out, columns_got, q_shard, o_shard, send, recv, local,
+    middle, stage, turned, columns_out, columns_got, q_shard, o_shard,
+    q_full, o_full, normed, q_ref, k_ref, v_ref, attended, lse_ref, cos, sin, send, recv, local,
 ):
     near = Neighbours(inner)
     copies = Copies(send, recv, local)
@@ -926,6 +928,21 @@
         copies.remote(
             lambda: (pairs.at[c] if k == 0 else near_hbm.at[c, k - 1], far_hbm.at[c, k]),
             ("f", c, k), ("f", c, k), near.over_y,
+        )
+
+    def far_one(c):
+        copies.arrived(far_hbm.at[c, 0], ("f", c, 0), near.over_y)
+        copies.remote(
+            lambda: (far_hbm.at[c, 0], far_hbm.at[c, 1]), ("fup", c), ("f", c, 1), near.along[2]
+        )
+        copies.remote(
+            lambda: (far_hbm.at[c, 0], far_hbm.at[c, 2]), ("fdown", c), ("f", c, 2), near.along[1]
+        )
+
+    def far_two(c):
+        copies.arrived(far_hbm.at[c, 1], ("f", c, 1), near.along[1])
+        copies.remote(
+            lambda: (far_hbm.at[c, 1], far_hbm.at[c, 3]), ("ftwo", c), ("f", c, 3), near.along[2]
         )
 
     def ring_got(c, k):
@@ -985,6 +1002,9 @@
     wide = pieces.astype(F32)
     summed = wide + roll_left(wide, each) + roll_left(wide, 2 * each)
     small[...] = summed.T[: small.shape[0], :]
+    copies.copy(lambda: (q_full, q_full_out), "q full")
+    copies.copy(lambda: (cos, cos_out), "cos")
+    copies.copy(lambda: (sin, sin_out), "sin")
     swapped(0)
     ring_one(0)
     over_y(0, 0)
@@ -1025,10 +1045,17 @@
         def _():
             gather_o.spread(2)
             gather_o.cross(0)
+            swapped(1)
+            ring_one(1)
+            over_y(1, 0)
 
         return carry
 
     lax.fori_loop(0, tiles, project, 0)
+    copies.copy(lambda: (normed, normed_out), "normed")
+    copies.copy(lambda: (q_ref, q_out), "q")
+    copies.copy(lambda: (k_ref, k_out), "k")
+    copies.copy(lambda: (v_ref, v_out), "v")
     for j in range(kv_slabs):
         lanes = slice(j * LANES, (j + 1) * LANES)
         spread_heads(k_ref[:, lanes], k_low, k_high, 2 * j)
@@ -1065,13 +1092,8 @@
 
         @pl.when(g == 1)
         def _():
-            ring_two(0)
-            over_y(0, 1)
             ring_got(0, 2)
             over_y(0, 2)
-            swapped(1)
-            ring_one(1)
-            over_y(1, 0)
             copies.remote(
                 lambda: (og_hbm.at[own_half], og_pair.at[mine]), ("og",), ("og",), near.over_x
             )
@@ -1079,22 +1101,24 @@
         @pl.when(g == 2)
         def _():
             gather_o.cross(3)
+            ring_two(0)
+            over_y(0, 1)
 
         @pl.when(g == 4)
         def _():
             gather_o.end()
-
-        @pl.when(g == slabs - 1)
-        def _():
-            ring_got(0, 3)
-            over_y(0, 3)
             swapped(2)
             ring_one(2)
             over_y(2, 0)
+            ring_got(0, 3)
+            over_y(0, 3)
 
         return carry
 
     lax.fori_loop(0, slabs, attend, 0)
+    copies.copy(lambda: (o_full, o_full_out), "o full")
+    copies.copy(lambda: (attended, attended_out), "attended")
+    copies.copy(lambda: (lse_ref, lse_out), "lse")
 
     def project_out(step, carry):
         tile = (step + 2 * (1 - core)) % tiles
@@ -1163,10 +1187,10 @@
             swapped(3)
             copies.copy(lambda: (pairs, pairs_hbm), "pairs")
         if step == 1:
-            ring_two(1)
-            over_y(1, 1)
-            ring_got(1, 2)
-            over_y(1, 2)
+            far_one(1)
+            far_two(1)
+        if step == 2:
+            ring_two(2)
 
     shares = experts // 2
     flipped = combine[...].T
@@ -1175,9 +1199,6 @@
     columns_out[...] = gone
     copies.remote(lambda: (columns_out, columns_got), ("c",), ("c",), near.over_x)
     combine_pair[:tokens, :] = kept.T
-    ring_two(2)
-    ring_got(1, 3)
-    over_y(1, 3)
 
     copies.arrived(og_pair.at[mine], ("og",), near.over_x)
     copies.remote(lambda: (og_pair.at[mine],) * 2, ("og2",), ("og2",), near.twin)
@@ -1236,13 +1257,18 @@
             lambda there=there, side=side: (turned.at[side], xt_hbm.at[:, there]),
             ("xgt", step), False,
         )
+    ring_two(1)
     for wait in waits + middle_out:
         wait()
+    ring_got(1, 2)
+    ring_got(1, 3)
     ring_got(2, 2)
     ring_got(2, 3)
-    for c in range(LATE + 1):
-        for k in range(SLOTS if c < LATE else 1):
-            copies.arrived(far_hbm.at[c, k], ("f", c, k), near.over_y)
+    for k in range(SLOTS):
+        copies.arrived(far_hbm.at[0, k], ("f", 0, k), near.over_y)
+    for k in (2, 3):
+        copies.arrived(far_hbm.at[1, k], ("f", 1, k), near.along[k])
+    copies.arrived(far_hbm.at[2, 0], ("f", 2, 0), near.over_y)
     copies.finish()
 
 
@@ -1259,25 +1285,28 @@
     shape = jax.ShapeDtypeStruct
     inner = lax.axis_size("dp") // 16
     dma = pltpu.SemaphoreType.DMA
+    kept = [
+        shape((16, block, q_columns), BF16),
+        shape((16, block, q_width), BF16),
+        shape((width, tokens), BF16),
+        shape((tokens, q_width), BF16),
+        shape((tokens, kv_width), BF16),
+        shape((tokens, kv_width), BF16),
+        shape((tokens, q_width), BF16),
+        shape((slabs, 8, tokens), F32),
+        shape((tokens, LANES), F32),
+        shape((tokens, LANES), F32),
+    ]
     return pl.pallas_call(
         functools.partial(forward_kernel, inner),
         in_specs=[vmem] * 8 + [anywhere] * 4,
-        out_specs=[vmem] * 14 + [anywhere] * 8,
+        out_specs=[vmem] * 4 + [anywhere] * 18,
         out_shape=[
-            shape((16, block, q_columns), BF16),
-            shape((16, block, q_width), BF16),
             shape((24, width), F32),
-            shape((width, tokens), BF16),
-            shape((tokens, q_width), BF16),
-            shape((tokens, kv_width), BF16),
-            shape((tokens, kv_width), BF16),
-            shape((tokens, q_width), BF16),
-            shape((slabs, 8, tokens), F32),
             shape((tokens, LANES), F32),
             shape((2 * tokens, experts // 2), F32),
-            shape((tokens, LANES), F32),
-            shape((tokens, LANES), F32),
             shape((tokens, 1), F32),
+            *kept,
             shape((tokens, width), F32),
             shape((2 * tokens, width), BF16),
             shape((width, 2 * tokens), BF16),
@@ -1305,7 +1334,8 @@
             pltpu.VMEM((experts // 2, tokens), F32),
             pltpu.VMEM((block, q_columns), BF16),
             pltpu.VMEM((block, q_width), BF16),
-            dma((80,)), dma((80,)), dma((60,)),
+            *[pltpu.VMEM(one.shape, one.dtype) for one in kept],
+            dma((80,)), dma((80,)), dma((64,)),
         ],
         compiler_params=pltpu.CompilerParams(
             vmem_limit_bytes=EXPERT_VMEM, collective_id=1, has_side_effects=True
@@ -1385,8 +1415,8 @@
 
 def backward_kernel(
     inner,
-    o_full, q_ref, k_ref, v_ref, attended, lse_ref, cos, sin, seg_col, seg_row, small, combine,
-    gate_turned, q_hbm, normed_hbm, hidden_hbm, og_hbm, middle_hbm, dx_own, dx_twin, dx_other,
+    seg_col, seg_row, small, combine, gate_turned,
+    o_full_hbm, attended_hbm, q_ref_hbm, k_ref_hbm, v_ref_hbm, lse_hbm, cos_hbm, sin_hbm, q_hbm, normed_hbm, hidden_hbm, og_hbm, middle_hbm, dx_own, dx_twin, dx_other,
     mix_pair, *refs,
 ):
     keeps, refs = refs[:SENT], refs[SENT:]
@@ -1398,6 +1428,7 @@
         attended_grad, lin_grad, o_grad, q_grad, o_one, o_two, o_y, o_x, o_z,
         q_one, q_two, q_y, q_x, q_z, part_got, pieces, z_send, z_keep, given, kept,
         strips, wide_in, wide_out, strip_out, router_rows, gate_columns, small_sum,
+        o_full, attended, q_ref, k_ref, v_ref, lse_ref, cos, sin,
         send, recv, local, strip_sem, wide_sem, out_sem,
     ) = refs[18:]
     near = Neighbours(inner)
@@ -1533,6 +1564,17 @@
 
     for i, k in enumerate((1, 2)):
         y_load(SENT, k, i, (0, 1))
+    weights_in = copies.copy(lambda: (o_full_hbm, o_full), "o full", False)
+    attended_in = copies.copy(lambda: (attended_hbm, attended), "attended", False)
+    operands_in = [
+        copies.copy(lambda one=one, to=to: (one, to), ("operand", i), False)
+        for i, (one, to) in enumerate(
+            (
+                (q_ref_hbm, q_ref), (k_ref_hbm, k_ref), (v_ref_hbm, v_ref), (lse_hbm, lse_ref),
+                (cos_hbm, cos), (sin_hbm, sin),
+            )
+        )
+    ]
     near.greet()
     for k in (1, 2, 3, 0):
         copies.remote(
@@ -1617,7 +1659,9 @@
                 a[:e] + a[e : 2 * e] + a[2 * e :] + b[:e] + b[e : 2 * e] + c[:e]
             )
 
+        weights_in()
         over_strips([dx_own, dx_twin, dx_other, og_hbm], middle_hbm, wide_out, mid_grad, compute)
+        attended_in()
         for group in range(SLOTS):
             rows = slice(4 * block * group, 4 * block * (group + 1))
             o_grad[4 * group : 4 * (group + 1)] = (
@@ -1630,6 +1674,8 @@
 
     def attention_part(bias0, bias1, bias2, bias3, k_low, k_high, v_low, v_high, dk, dv, dq):
         biases = (bias0, bias1, bias2, bias3)
+        for wait in operands_in:
+            wait()
         for at, bias in enumerate(biases):
             upto = bias.shape[0]
             keys_at = lax.broadcasted_iota(jnp.int32, bias.shape, 0)
@@ -1862,12 +1908,10 @@
             pltpu.VMEM((SLOTS - 1, block, total), BF16),
         ]
 
-    values = (
-        o_full, q, k, v, attended, lse, cosine, sine, seg_col, segments[None, :],
-        small, combine, gate_turned,
-    )
+    values = (seg_col, segments[None, :], small, combine, gate_turned)
+    read = (o_full, attended, q, k, v, lse, cosine, sine)
     far_values = (
-        q_full, normed, hidden, og, middle, *dx, mix, *keep, *parts, *near_grads, *far_grads,
+        *read, q_full, normed, hidden, og, middle, *dx, mix, *keep, *parts, *near_grads, *far_grads,
     )
     return pl.pallas_call(
         functools.partial(backward_kernel, inner),
@@ -1910,7 +1954,8 @@
             pltpu.VMEM((LANES, width), BF16),
             pltpu.VMEM((tokens, LANES), F32),
             pltpu.VMEM((8 + experts, width), F32),
-            dma((80,)), dma((80,)), dma((60,)), dma((4, 2)), dma((2,)), dma((2,)),
+            *[pltpu.VMEM(one.shape, one.dtype) for one in read],
+            dma((80,)), dma((80,)), dma((64,)), dma((4, 2)), dma((2,)), dma((2,)),
         ],
         compiler_params=pltpu.CompilerParams(
             vmem_limit_bytes=EXPERT_VMEM, collective_id=2, has_side_effects=True
@@ -2357,8 +2402,8 @@
         inner_gather(turned_out[0], 0), inner_gather(w_router, 0), inner_gather(norm_gains, 1),
     )
     (
-        qkv_blocks, out_blocks, small, normed_low, queries, keys, values, attended, lse,
-        combine, combine_pair, cosine, sine, seg_col,
+        small, combine, combine_pair, seg_col,
+        qkv_blocks, out_blocks, normed_low, queries, keys, values, attended, lse, cosine, sine,
         middle, x_pair, x_turned, og_pair, og_turned, pairs, near, far,
     ) = forward_pass(
         weights, frequency, segments, routes, gateup_rows, down_rows, hidden_in, out_grad

time: 632 us -> 641 us (1.014)
    pallas_call x1, Pallas kernels: 190 us -> 207 us  [forward_pass(): pl.pallas_call(functools.partial(forward_kernel, inner), in_specs=[vmem]...]
    pallas_call x1, Pallas kernels: 184 us -> 171 us  [backward_pass(): pl.pallas_call(functools.partial(backward_kernel, inner), in_specs=[vmem]...]
where the time goes in v1:
time: 641 us; the launch traced here: 631 us
  Pallas kernels  602 us (94%)
  starting transfers between devices  12.7 us (2%)
  local copies, waits for them, and re-layouts  12.2 us (2%)
    pallas_call x1, Pallas kernels, forward_pass(): pl.pallas_call(functools.partial(forward_kernel, inner), in_specs=[vmem]...  207 us
    pallas_call x1, Pallas kernels, experts_pass(): pl.pallas_call(functools.partial(experts_kernel, inner, chunks, row_steps...  205 us
    pallas_call x1, Pallas kernels, backward_pass(): pl.pallas_call(functools.partial(backward_kernel, inner), in_specs=[vmem]...  171 us
    pallas_call x1, Pallas kernels, adam_experts(): pl.pallas_call(adam_experts_kernel, grid=(experts // CHUNK,), in_specs=[s...  15.1 us
  transfers between devices with their start and end apart: 1, of which 0 were waited for; matrix products, arithmetic and copies ran while one was open for 1% of the time, Pallas kernels for 2%

profile of v1, /device:TPU:3, one launch (start us, length us, event | category | flops | bytes accessed | tf_op | source)
XLA Modules:
  0.0 631.2 jit_solution(8555990602578419042)
XLA Ops:
  0.7 1.4 copy.70.w_router
  2.1 0.6 maximum_bitcast_fusion.frequency
  2.7 206.9 %forward_pass.1 = (f32[24,1536]{1,0:T(8,128)}, f32[1024,128]{1,0:T(8,128)}, f32[2048,8]{1,0:T(8,128)}, f32[1024,1]{1,0:T(8,128)}, bf16[16,96,1408]{2,1,0:T(8,128...) custom-call(f32[96,768]{1,0:T(8,128)} %refs_2_.2, ...), custom_call_target="tpu_custom_call" | custom-call | tf_op jit(solution)/shard_map/forward_pass/pallas_call | solution.py:1300
  209.6 205.4 %experts_pass.1 = (bf16[1024,1536]{1,0:T(8,128)(2,1)}, bf16[1024,1536]{1,0:T(8,128)(2,1)}, bf16[1024,1536]{1,0:T(8,128)(2,1)}, bf16[2048,1536]{1,0:T(8,128)(2,1)...) custom-call(bf16[2048,1536]{1,0:T(8,128)(2,1)} %get-tuple-element.84, ...), custom_call_target="tpu_custom_call" | custom-call | flops 154618822656 | bytes 18874368 | tf_op jit(solution)/shard_map/experts_pass/pallas_call | solution.py:642
  415.0 171.0 %backward_pass.1 = (f32[96,1408]{1,0:T(8,128)}, f32[96,768]{1,0:T(8,128)}, f32[1024,1536]{1,0:T(8,128)}, bf16[1024,1536]{1,0:T(8,128)(2,1)}, f32[4,96,1536]{2,1,...) custom-call(f32[1024,1]{1,0:T(8,128)} %get-tuple-element.81.seg_col,, ...), custom_call_target="tpu_custom_call" | custom-call | tf_op jit(solution)/shard_map/backward_pass/pallas_call | solution.py:1916
  586.0 0.0 copy-start.2
  586.0 0.0 copy-start.3
  586.1 0.0 copy-start.4
  586.1 0.0 copy-start.1
  586.1 3.7 adam_attention.1
  589.8 0.9 reduce
  590.7 12.7 %collective-permute-start = (f32[1,96]{1,0:T(1,128)S(1)}, f32[1,96]{1,0:T(1,128)S(1)}, u32[]{:S(2)}, u32[]{:S(2)}) collective-permute-start(f32[1,96]{1,0:T(1,128)S(1)} %bitcast.32), channel_id=1, source_target_pairs={{0,1},{1,0},{2,3},{3,2},{4,5},{5,4},{6,7},{7,6},{8,9},{9,8},{10,11... | collective-permute-start | bytes 1160 | tf_op jit(solution)/shard_map/ppermute | solution.py:2328
  603.4 0.9 slice_reduce_fusion
  604.3 0.0 copy-done.2
  604.4 0.0 copy-done.3
  604.4 0.1 copy.72
  604.5 0.0 copy-done.4
  604.5 0.1 copy.73
  604.6 0.1 copy.74
  604.7 0.0 copy-done.1
  604.7 0.9 multiply_subtract_fusion
  605.6 0.7 copy.76
  606.3 0.7 copy.77
  606.9 0.7 copy.78
  607.6 0.0 copy-start.5
  607.6 0.0 copy-start.6
  607.6 0.0 copy-start.7
  607.6 0.0 copy-start
  607.6 15.1 %adam_experts.1 = (f32[16,2,96,256]{3,2,1,0:T(8,128)}, f32[16,2,96,256]{3,2,1,0:T(8,128)}, f32[16,2,96,256]{3,2,1,0:T(8,128)}, f32[16,96,256]{2,1,0:T(8,128)}, f...) custom-call(s32[1]{0:T(128)} %bitcast.10.x_at, f32[4,96,1536]{2,1,0:T(8,128)} %get-tuple-element.131.kept, ...), custom_call_target="tpu_custom_call" | custom-call | tf_op jit(solution)/shard_map/adam_experts/pallas_call | solution.py:2117
  622.7 0.0 collective-permute-done
  622.7 0.0 copy-done.5
  622.8 0.0 copy-done.6
  622.8 0.0 copy-done.7
  622.8 0.6 multiply_subtract_fusion.1
  623.4 0.0 copy-done
  623.4 1.7 copy.81
  625.0 5.9 copy.82
  (5 shorter events, 0.0 us)
Async XLA Ops:
  586.0 18.3 %copy-start.2 = (f32[96,16]{0,1:T(8,128)S(1)}, f32[96,16]{0,1:T(8,128)}, u32[]{:S(2)}) copy-start(f32[96,16]{0,1:T(8,128)} %param.41) | copy-start | bytes 18436
  586.0 18.3 %copy-start.3 = (f32[96,16]{0,1:T(8,128)S(1)}, f32[96,16]{0,1:T(8,128)}, u32[]{:S(2)}) copy-start(f32[96,16]{0,1:T(8,128)} %param.42) | copy-start | bytes 18436
  586.1 18.4 %copy-start.4 = (f32[96,16]{0,1:T(8,128)S(1)}, f32[96,16]{0,1:T(8,128)}, u32[]{:S(2)}) copy-start(f32[96,16]{0,1:T(8,128)} %param.43) | copy-start | bytes 18436
  586.1 18.6 %copy-start.1 = (f32[96,16]{1,0:T(8,128)S(1)}, f32[96,16]{1,0:T(8,128)}, u32[]{:S(2)}) copy-start(f32[96,16]{1,0:T(8,128)} %copy.70.w_router) | copy-start | bytes 18436
  590.7 32.0 %collective-permute-start = (f32[1,96]{1,0:T(1,128)S(1)}, f32[1,96]{1,0:T(1,128)S(1)}, u32[]{:S(2)}, u32[]{:S(2)}) collective-permute-start(f32[1,96]{1,0:T(1,128)S(1)} %bitcast.32), channel_id=1, source_target_pairs={{0,1},{1,0},{2,3},{3,2},{4,5},{5,4},{6,7},{7,6},{8,9},{9,8},{10,11... | collective-permute-start | bytes 1160 | tf_op jit(solution)/shard_map/ppermute | solution.py:2328
  607.6 15.1 %copy-start.5 = (f32[2,96]{1,0:T(2,128)S(1)}, f32[2,96]{1,0:T(2,128)}, u32[]{:S(2)}) copy-start(f32[2,96]{1,0:T(2,128)} %gains.1) | copy-start | bytes 2308
  607.6 15.2 %copy-start.6 = (f32[2,96]{1,0:T(2,128)S(1)}, f32[2,96]{1,0:T(2,128)}, u32[]{:S(2)}) copy-start(f32[2,96]{1,0:T(2,128)} %param.31) | copy-start | bytes 2308
  607.6 15.2 %copy-start.7 = (f32[2,96]{1,0:T(2,128)S(1)}, f32[2,96]{1,0:T(2,128)}, u32[]{:S(2)}) copy-start(f32[2,96]{1,0:T(2,128)} %param.30) | copy-start | bytes 2308
  607.6 15.8 %copy-start = (bf16[1024,1536]{1,0:T(8,128)(2,1)S(1)}, bf16[1024,1536]{1,0:T(8,128)(2,1)}, u32[]{:S(2)}) copy-start(bf16[1024,1536]{1,0:T(8,128)(2,1)} %get-tuple-element.237) | copy-start | bytes 9437188

commit v2 on v1

--- a/solution.py
+++ b/solution.py
@@ -425,11 +425,11 @@
                 ("part", c, k), ("part", c, BACK[k]), near.along[k],
             )
 
-    @pl.when(step == 2 * steps + 3)
+    @pl.when(step == 2 * steps + 1)
     def _():
         add_arrived(0)
 
-    @pl.when(step == 3 * steps + 3)
+    @pl.when(step == 3 * steps + 2)
     def _():
         add_arrived(1)
 
@@ -930,21 +930,6 @@
             ("f", c, k), ("f", c, k), near.over_y,
         )
 
-    def far_one(c):
-        copies.arrived(far_hbm.at[c, 0], ("f", c, 0), near.over_y)
-        copies.remote(
-            lambda: (far_hbm.at[c, 0], far_hbm.at[c, 1]), ("fup", c), ("f", c, 1), near.along[2]
-        )
-        copies.remote(
-            lambda: (far_hbm.at[c, 0], far_hbm.at[c, 2]), ("fdown", c), ("f", c, 2), near.along[1]
-        )
-
-    def far_two(c):
-        copies.arrived(far_hbm.at[c, 1], ("f", c, 1), near.along[1])
-        copies.remote(
-            lambda: (far_hbm.at[c, 1], far_hbm.at[c, 3]), ("ftwo", c), ("f", c, 3), near.along[2]
-        )
-
     def ring_got(c, k):
         copies.arrived(near_hbm.at[c, k - 1], ("r", c, k), near.along[k])
 
@@ -1045,9 +1030,6 @@
         def _():
             gather_o.spread(2)
             gather_o.cross(0)
-            swapped(1)
-            ring_one(1)
-            over_y(1, 0)
 
         return carry
 
@@ -1092,8 +1074,13 @@
 
         @pl.when(g == 1)
         def _():
+            ring_two(0)
+            over_y(0, 1)
             ring_got(0, 2)
             over_y(0, 2)
+            swapped(1)
+            ring_one(1)
+            over_y(1, 0)
             copies.remote(
                 lambda: (og_hbm.at[own_half], og_pair.at[mine]), ("og",), ("og",), near.over_x
             )
@@ -1101,17 +1088,18 @@
         @pl.when(g == 2)
         def _():
             gather_o.cross(3)
-            ring_two(0)
-            over_y(0, 1)
 
         @pl.when(g == 4)
         def _():
             gather_o.end()
+
+        @pl.when(g == slabs - 1)
+        def _():
+            ring_got(0, 3)
+            over_y(0, 3)
             swapped(2)
             ring_one(2)
             over_y(2, 0)
-            ring_got(0, 3)
-            over_y(0, 3)
 
         return carry
 
@@ -1187,10 +1175,10 @@
             swapped(3)
             copies.copy(lambda: (pairs, pairs_hbm), "pairs")
         if step == 1:
-            far_one(1)
-            far_two(1)
-        if step == 2:
-            ring_two(2)
+            ring_two(1)
+            over_y(1, 1)
+            ring_got(1, 2)
+            over_y(1, 2)
 
     shares = experts // 2
     flipped = combine[...].T
@@ -1199,6 +1187,9 @@
     columns_out[...] = gone
     copies.remote(lambda: (columns_out, columns_got), ("c",), ("c",), near.over_x)
     combine_pair[:tokens, :] = kept.T
+    ring_two(2)
+    ring_got(1, 3)
+    over_y(1, 3)
 
     copies.arrived(og_pair.at[mine], ("og",), near.over_x)
     copies.remote(lambda: (og_pair.at[mine],) * 2, ("og2",), ("og2",), near.twin)
@@ -1257,18 +1248,13 @@
             lambda there=there, side=side: (turned.at[side], xt_hbm.at[:, there]),
             ("xgt", step), False,
         )
-    ring_two(1)
     for wait in waits + middle_out:
         wait()
-    ring_got(1, 2)
-    ring_got(1, 3)
     ring_got(2, 2)
     ring_got(2, 3)
-    for k in range(SLOTS):
-        copies.arrived(far_hbm.at[0, k], ("f", 0, k), near.over_y)
-    for k in (2, 3):
-        copies.arrived(far_hbm.at[1, k], ("f", 1, k), near.along[k])
-    copies.arrived(far_hbm.at[2, 0], ("f", 2, 0), near.over_y)
+    for c in range(LATE + 1):
+        for k in range(SLOTS if c < LATE else 1):
+            copies.arrived(far_hbm.at[c, k], ("f", c, k), near.over_y)
     copies.finish()
 
 

time: 641 us -> 625 us (0.975)
  Pallas kernels: 602 us -> 591 us
    pallas_call x1, Pallas kernels: 207 us -> 185 us  [forward_pass(): pl.pallas_call(functools.partial(forward_kernel, inner), in_specs=[vmem]...]
where the time goes in v2:
time: 625 us; the launch traced here: 617 us
  Pallas kernels  591 us (95%)
  local copies, waits for them, and re-layouts  12.2 us (2%)
  starting transfers between devices  9.44 us (2%)
    pallas_call x1, Pallas kernels, experts_pass(): pl.pallas_call(functools.partial(experts_kernel, inner, chunks, row_steps...  211 us
    pallas_call x1, Pallas kernels, forward_pass(): pl.pallas_call(functools.partial(forward_kernel, inner), in_specs=[vmem]...  185 us
    pallas_call x1, Pallas kernels, backward_pass(): pl.pallas_call(functools.partial(backward_kernel, inner), in_specs=[vmem]...  176 us
    pallas_call x1, Pallas kernels, adam_experts(): pl.pallas_call(adam_experts_kernel, grid=(experts // CHUNK,), in_specs=[s...  15.1 us
  transfers between devices with their start and end apart: 1, of which 0 were waited for; matrix products, arithmetic and copies ran while one was open for 1% of the time, Pallas kernels for 2%

profile of v2, /device:TPU:3, one launch (start us, length us, event | category | flops | bytes accessed | tf_op | source)
XLA Modules:
  0.0 616.7 jit_solution(10234747259787291869)
XLA Ops:
  0.7 1.4 copy.70.w_router
  2.1 0.6 maximum_bitcast_fusion.frequency
  2.7 185.1 %forward_pass.1 = (f32[24,1536]{1,0:T(8,128)}, f32[1024,128]{1,0:T(8,128)}, f32[2048,8]{1,0:T(8,128)}, f32[1024,1]{1,0:T(8,128)}, bf16[16,96,1408]{2,1,0:T(8,128...) custom-call(f32[96,768]{1,0:T(8,128)} %refs_2_.2, ...), custom_call_target="tpu_custom_call" | custom-call | tf_op jit(solution)/shard_map/forward_pass/pallas_call | solution.py:1286
  187.8 211.3 %experts_pass.1 = (bf16[1024,1536]{1,0:T(8,128)(2,1)}, bf16[1024,1536]{1,0:T(8,128)(2,1)}, bf16[1024,1536]{1,0:T(8,128)(2,1)}, bf16[2048,1536]{1,0:T(8,128)(2,1)...) custom-call(bf16[2048,1536]{1,0:T(8,128)(2,1)} %get-tuple-element.84, ...), custom_call_target="tpu_custom_call" | custom-call | flops 154618822656 | bytes 18874368 | tf_op jit(solution)/shard_map/experts_pass/pallas_call | solution.py:642
  399.1 175.7 %backward_pass.1 = (f32[96,1408]{1,0:T(8,128)}, f32[96,768]{1,0:T(8,128)}, f32[1024,1536]{1,0:T(8,128)}, bf16[1024,1536]{1,0:T(8,128)(2,1)}, f32[4,96,1536]{2,1,...) custom-call(f32[1024,1]{1,0:T(8,128)} %get-tuple-element.81.seg_col,, ...), custom_call_target="tpu_custom_call" | custom-call | tf_op jit(solution)/shard_map/backward_pass/pallas_call | solution.py:1902
  574.8 0.0 copy-start.2
  574.8 0.0 copy-start.3
  574.8 0.0 copy-start.4
  574.8 0.0 copy-start.1
  574.8 3.7 adam_attention.1
  578.6 0.9 reduce
  579.5 9.4 %collective-permute-start = (f32[1,96]{1,0:T(1,128)S(1)}, f32[1,96]{1,0:T(1,128)S(1)}, u32[]{:S(2)}, u32[]{:S(2)}) collective-permute-start(f32[1,96]{1,0:T(1,128)S(1)} %bitcast.32), channel_id=1, source_target_pairs={{0,1},{1,0},{2,3},{3,2},{4,5},{5,4},{6,7},{7,6},{8,9},{9,8},{10,11... | collective-permute-start | bytes 1160 | tf_op jit(solution)/shard_map/ppermute | solution.py:2314
  588.9 0.9 slice_reduce_fusion
  589.8 0.0 copy-done.2
  589.8 0.0 copy-done.3
  589.9 0.1 copy.72
  589.9 0.0 copy-done.4
  590.0 0.1 copy.73
  590.1 0.1 copy.74
  590.1 0.0 copy-done.1
  590.2 0.9 multiply_subtract_fusion
  591.1 0.7 copy.76
  591.7 0.7 copy.77
  592.4 0.7 copy.78
  593.1 0.0 copy-start.5
  593.1 0.0 copy-start.6
  593.1 0.0 copy-start.7
  593.1 0.0 copy-start
  593.1 15.1 %adam_experts.1 = (f32[16,2,96,256]{3,2,1,0:T(8,128)}, f32[16,2,96,256]{3,2,1,0:T(8,128)}, f32[16,2,96,256]{3,2,1,0:T(8,128)}, f32[16,96,256]{2,1,0:T(8,128)}, f...) custom-call(s32[1]{0:T(128)} %bitcast.10.x_at, f32[4,96,1536]{2,1,0:T(8,128)} %get-tuple-element.131.kept, ...), custom_call_target="tpu_custom_call" | custom-call | tf_op jit(solution)/shard_map/adam_experts/pallas_call | solution.py:2103
  608.2 0.0 collective-permute-done
  608.2 0.0 copy-done.5
  608.2 0.0 copy-done.6
  608.3 0.0 copy-done.7
  608.3 0.6 multiply_subtract_fusion.1
  608.9 0.0 copy-done
  608.9 1.7 copy.81
  610.5 5.9 copy.82
  (5 shorter events, 0.0 us)
Async XLA Ops:
  574.8 15.0 %copy-start.2 = (f32[96,16]{0,1:T(8,128)S(1)}, f32[96,16]{0,1:T(8,128)}, u32[]{:S(2)}) copy-start(f32[96,16]{0,1:T(8,128)} %param.41) | copy-start | bytes 18436
  574.8 15.0 %copy-start.3 = (f32[96,16]{0,1:T(8,128)S(1)}, f32[96,16]{0,1:T(8,128)}, u32[]{:S(2)}) copy-start(f32[96,16]{0,1:T(8,128)} %param.42) | copy-start | bytes 18436
  574.8 15.1 %copy-start.4 = (f32[96,16]{0,1:T(8,128)S(1)}, f32[96,16]{0,1:T(8,128)}, u32[]{:S(2)}) copy-start(f32[96,16]{0,1:T(8,128)} %param.43) | copy-start | bytes 18436
  574.8 15.3 %copy-start.1 = (f32[96,16]{1,0:T(8,128)S(1)}, f32[96,16]{1,0:T(8,128)}, u32[]{:S(2)}) copy-start(f32[96,16]{1,0:T(8,128)} %copy.70.w_router) | copy-start | bytes 18436
  579.5 28.7 %collective-permute-start = (f32[1,96]{1,0:T(1,128)S(1)}, f32[1,96]{1,0:T(1,128)S(1)}, u32[]{:S(2)}, u32[]{:S(2)}) collective-permute-start(f32[1,96]{1,0:T(1,128)S(1)} %bitcast.32), channel_id=1, source_target_pairs={{0,1},{1,0},{2,3},{3,2},{4,5},{5,4},{6,7},{7,6},{8,9},{9,8},{10,11... | collective-permute-start | bytes 1160 | tf_op jit(solution)/shard_map/ppermute | solution.py:2314
  593.1 15.1 %copy-start.5 = (f32[2,96]{1,0:T(2,128)S(1)}, f32[2,96]{1,0:T(2,128)}, u32[]{:S(2)}) copy-start(f32[2,96]{1,0:T(2,128)} %gains.1) | copy-start | bytes 2308
  593.1 15.2 %copy-start.6 = (f32[2,96]{1,0:T(2,128)S(1)}, f32[2,96]{1,0:T(2,128)}, u32[]{:S(2)}) copy-start(f32[2,96]{1,0:T(2,128)} %param.31) | copy-start | bytes 2308
  593.1 15.2 %copy-start.7 = (f32[2,96]{1,0:T(2,128)S(1)}, f32[2,96]{1,0:T(2,128)}, u32[]{:S(2)}) copy-start(f32[2,96]{1,0:T(2,128)} %param.30) | copy-start | bytes 2308
  593.1 15.8 %copy-start = (bf16[1024,1536]{1,0:T(8,128)(2,1)S(1)}, bf16[1024,1536]{1,0:T(8,128)(2,1)}, u32[]{:S(2)}) copy-start(bf16[1024,1536]{1,0:T(8,128)(2,1)} %get-tuple-element.237) | copy-start | bytes 9437188

commit v3 on v2

--- a/solution.py
+++ b/solution.py
@@ -11,7 +11,6 @@
 QUERY_HEADS = 24
 HEAD_DIM = 64
 F = 512
-SEQUENCE_LENGTH = 1024
 STEP = 10
 
 NORM_EPSILON = 1e-06
@@ -24,7 +23,6 @@
 WEIGHT_DECAY = 0.1
 GAIN_RATE = 0.6
 MASK_VALUE = -1e30
-HIGHEST_PRECISION = lax.Precision.HIGHEST
 
 BF16 = jnp.bfloat16
 F32 = jnp.float32
@@ -39,24 +37,6 @@
 
 def dot(a, b, dims=NN):
     return lax.dot_general(a, b, dims, preferred_element_type=F32)
-
-
-def seq_positions(segment_row):
-    counter = jnp.arange(segment_row.shape[0], dtype=jnp.int32)
-    earlier = jnp.concatenate([segment_row[:1] - 1, segment_row[:-1]])
-    starts = lax.cummax(jnp.where(segment_row != earlier, counter, 0), axis=0)
-    return counter - starts
-
-
-def rope_tables(positions):
-    half_width = HEAD_DIM // 2
-    frequency = ROPE_BASE ** (-2.0 * jnp.arange(half_width, dtype=F32) / HEAD_DIM)
-    angles = positions.astype(F32)[:, None] * frequency[None, :]
-    cosine, sine = jnp.cos(angles), jnp.sin(angles)
-    return (
-        jnp.concatenate([cosine] * 4, axis=1),
-        jnp.concatenate([-sine, sine] * 2, axis=1),
-    )
 
 
 def rotate_halves(slab):
@@ -105,203 +85,6 @@
 
 def any_specs(arrays):
     return [pl.BlockSpec(memory_space=pl.ANY)] * len(arrays)
-
-
-def attention_forward_kernel(
-    lin_ref, kv_ref, cos_ref, sin_ref, seg_col, seg_row,
-    out_ref, q_ref, k_ref, v_ref, lse_ref,
-    bias, k_low, k_high, v_low, v_high,
-):
-    slab_at = pl.program_id(0)
-    span = lin_ref.shape[0]
-    kv_slabs = kv_ref.shape[1] // (2 * LANES)
-
-    @pl.when(slab_at == 0)
-    def _():
-        fill_bias(bias, seg_col, seg_row)
-        for j in range(kv_slabs):
-            lanes = slice(j * LANES, (j + 1) * LANES)
-            lin = kv_ref[:, lanes]
-            keys = (lin * cos_ref[...] + rotate_halves(lin) * sin_ref[...]).astype(BF16)
-            k_ref[:, lanes] = keys
-            spread_heads(keys, k_low, k_high, 2 * j)
-            lanes = slice((kv_slabs + j) * LANES, (kv_slabs + j + 1) * LANES)
-            values = kv_ref[:, lanes].astype(BF16)
-            v_ref[:, slice(j * LANES, (j + 1) * LANES)] = values
-            spread_heads(values, v_low, v_high, 2 * j)
-
-    lin = lin_ref[...]
-    q_ref[...] = (lin * cos_ref[...] + rotate_halves(lin) * sin_ref[...]).astype(BF16)
-    kv_even, kv_odd = (2 * slab_at) // 3, (2 * slab_at + 1) // 3
-    for at in range(0, span, ROWS):
-        rows = slice(at, at + ROWS)
-        queries = q_ref[rows, :]
-        total = None
-        stats = []
-        for keys, values, kv_at in ((k_low, v_low, kv_even), (k_high, v_high, kv_odd)):
-            upto = at + ROWS
-            scores = dot(queries, keys[kv_at, :upto, :], NT) * SCORE_SCALE + bias[rows, :upto]
-            highest = jnp.max(scores, axis=1, keepdims=True)
-            weights = jnp.exp(scores - highest)
-            summed = jnp.sum(weights, axis=1, keepdims=True)
-            probability = (weights * (1.0 / summed)).astype(BF16)
-            part = dot(probability, values[kv_at, :upto, :])
-            total = part if total is None else total + part
-            stats.append(highest + jnp.log(summed))
-        out_ref[rows, :] = total.astype(BF16)
-        spread = jnp.where(half_mask(ROWS, False), stats[0], stats[1])
-        turned = spread.T
-        lse_ref[0, 0:1, rows] = turned[0:1, :]
-        lse_ref[0, 1:2, rows] = turned[HEAD_DIM : HEAD_DIM + 1, :]
-
-
-def attention_forward(qkv_lin, cosine, sine, segment_row, earlier=()):
-    span = qkv_lin.shape[0]
-    q_width = MODEL_DIM // 2
-    kv_width = (qkv_lin.shape[1] - q_width) // 2
-    slabs, kv_heads = q_width // LANES, kv_width // HEAD_DIM
-    whole = lambda shape: pl.BlockSpec(shape, lambda g: (0,) * len(shape))
-    slab = pl.BlockSpec((span, LANES), lambda g: (0, g))
-    q_lin, kv_lin = qkv_lin[:, :q_width], qkv_lin[:, q_width:]
-    return pl.pallas_call(
-        with_earlier(attention_forward_kernel, 6, len(earlier)),
-        grid=(slabs,),
-        in_specs=[
-            slab, whole((span, 2 * kv_width)), whole((span, LANES)), whole((span, LANES)),
-            whole((span, 1)), whole((1, span)),
-        ]
-        + any_specs(earlier),
-        out_specs=[
-            slab, slab, whole((span, kv_width)), whole((span, kv_width)),
-            pl.BlockSpec((1, 8, span), lambda g: (g, 0, 0)),
-        ],
-        out_shape=[
-            jax.ShapeDtypeStruct((span, q_width), BF16),
-            jax.ShapeDtypeStruct((span, q_width), BF16),
-            jax.ShapeDtypeStruct((span, kv_width), BF16),
-            jax.ShapeDtypeStruct((span, kv_width), BF16),
-            jax.ShapeDtypeStruct((slabs, 8, span), F32),
-        ],
-        scratch_shapes=[pltpu.VMEM((span, span), F32)]
-        + [pltpu.VMEM((kv_heads, span, LANES), BF16)] * 4,
-        compiler_params=pltpu.CompilerParams(vmem_limit_bytes=VMEM_BYTES),
-        cost_estimate=pl.CostEstimate(
-            flops=32 * slabs * span * span * LANES, bytes_accessed=16 * span * q_width,
-            transcendentals=slabs * span * span,
-        ),
-        name="attention_forward",
-    )(q_lin, kv_lin, cosine, sine, segment_row[:, None], segment_row[None, :], *earlier)
-
-
-def attention_backward_kernel(
-    q_ref, k_ref, v_ref, out_ref, grad_ref, cos_ref, sin_ref, seg_col, seg_row, lse_ref,
-    dq_ref, dkv_ref,
-    bias, k_low, k_high, v_low, v_high, dk_low, dk_high, dv_low, dv_high, dq_sum,
-):
-    slab_at = pl.program_id(0)
-    span = q_ref.shape[0]
-    kv_slabs = k_ref.shape[1] // LANES
-
-    @pl.when(slab_at == 0)
-    def _():
-        for at in range(0, span, ROWS):
-            keys_at = at + lax.broadcasted_iota(jnp.int32, (ROWS, span), 0)
-            rows_at = lax.broadcasted_iota(jnp.int32, (ROWS, span), 1)
-            allowed = (rows_at >= keys_at) & (seg_col[at : at + ROWS, :] == seg_row[...])
-            bias[at : at + ROWS, :] = jnp.where(allowed, 0.0, MASK_VALUE).astype(F32)
-        for j in range(kv_slabs):
-            lanes = slice(j * LANES, (j + 1) * LANES)
-            spread_heads(k_ref[:, lanes], k_low, k_high, 2 * j)
-            spread_heads(v_ref[:, lanes], v_low, v_high, 2 * j)
-        for sums in (dk_low, dk_high, dv_low, dv_high):
-            sums[...] = jnp.zeros_like(sums)
-
-    kv_even, kv_odd = (2 * slab_at) // 3, (2 * slab_at + 1) // 3
-    for at in range(0, span, ROWS):
-        rows = slice(at, at + ROWS)
-        upto = at + ROWS
-        queries, grads = q_ref[rows, :], grad_ref[rows, :]
-        turned = (grads.astype(F32) * out_ref[rows, :].astype(F32)).T
-        zero = jnp.zeros_like(queries)
-        dq_part = None
-        for upper, keys, values, dk_sum, dv_sum, kv_at in (
-            (False, k_low, v_low, dk_low, dv_low, kv_even),
-            (True, k_high, v_high, dk_high, dv_high, kv_odd),
-        ):
-            first = HEAD_DIM if upper else 0
-            delta = jnp.sum(turned[first : first + HEAD_DIM, :], axis=0, keepdims=True)
-            head = 1 if upper else 0
-            total = lse_ref[0, head : head + 1, rows]
-            keys_here = keys[kv_at, :upto, :]
-            scores = dot(keys_here, queries, NT) * SCORE_SCALE + bias[:upto, rows]
-            probability = jnp.exp(scores - total)
-            prob_grad = dot(values[kv_at, :upto, :], grads, NT)
-            score_grad = (probability * (prob_grad - delta)).astype(BF16)
-            mask = half_mask(ROWS, upper)
-            dv_sum[kv_at, :upto, :] += dot(
-                probability.astype(BF16), jnp.where(mask, grads, zero)
-            )
-            dk_sum[kv_at, :upto, :] += dot(score_grad, jnp.where(mask, queries, zero))
-            part = dot(score_grad, keys_here, TN)
-            dq_part = part if dq_part is None else dq_part + part
-        dq_sum[rows, :] = dq_part * SCORE_SCALE
-    slab = dq_sum[...]
-    dq_ref[...] = (slab * cos_ref[...] - rotate_halves(slab) * sin_ref[...]).astype(BF16)
-
-    @pl.when(slab_at == pl.num_programs(0) - 1)
-    def _():
-        low = half_mask(span, False)
-
-        def joined(sums_low, sums_high, j):
-            one = sums_low[2 * j] + pltpu.roll(sums_high[2 * j], HEAD_DIM, 1)
-            two = pltpu.roll(sums_low[2 * j + 1], HEAD_DIM, 1) + sums_high[2 * j + 1]
-            return jnp.where(low, one, two)
-
-        for j in range(kv_slabs):
-            slab = joined(dk_low, dk_high, j) * SCORE_SCALE
-            dkv_ref[:, j * LANES : (j + 1) * LANES] = (
-                slab * cos_ref[...] - rotate_halves(slab) * sin_ref[...]
-            ).astype(BF16)
-            at = (kv_slabs + j) * LANES
-            dkv_ref[:, at : at + LANES] = joined(dv_low, dv_high, j).astype(BF16)
-
-
-def attention_backward(
-    queries, keys, values, attended, grad, cosine, sine, segment_row, lse, earlier=()
-):
-    span, q_width = queries.shape
-    kv_width = keys.shape[1]
-    slabs, kv_heads = q_width // LANES, kv_width // HEAD_DIM
-    whole = lambda shape: pl.BlockSpec(shape, lambda g: (0,) * len(shape))
-    slab = pl.BlockSpec((span, LANES), lambda g: (0, g))
-    return pl.pallas_call(
-        with_earlier(attention_backward_kernel, 10, len(earlier)),
-        grid=(slabs,),
-        in_specs=[
-            slab, whole((span, kv_width)), whole((span, kv_width)), slab, slab,
-            whole((span, LANES)), whole((span, LANES)), whole((span, 1)), whole((1, span)),
-            pl.BlockSpec((1, 8, span), lambda g: (g, 0, 0)),
-        ]
-        + any_specs(earlier),
-        out_specs=[slab, whole((span, 2 * kv_width))],
-        out_shape=[
-            jax.ShapeDtypeStruct((span, q_width), BF16),
-            jax.ShapeDtypeStruct((span, 2 * kv_width), BF16),
-        ],
-        scratch_shapes=[pltpu.VMEM((span, span), F32)]
-        + [pltpu.VMEM((kv_heads, span, LANES), BF16)] * 4
-        + [pltpu.VMEM((kv_heads, span, LANES), F32)] * 4
-        + [pltpu.VMEM((span, LANES), F32)],
-        compiler_params=pltpu.CompilerParams(vmem_limit_bytes=VMEM_BYTES),
-        cost_estimate=pl.CostEstimate(
-            flops=40 * slabs * span * span * LANES, bytes_accessed=16 * span * q_width,
-            transcendentals=slabs * span * span,
-        ),
-        name="attention_backward",
-    )(
-        queries, keys, values, attended, grad, cosine, sine,
-        segment_row[:, None], segment_row[None, :], lse, *earlier,
-    )
 
 
 EXPERT_ROWS = 256
@@ -864,10 +647,9 @@
     q_shard[:, q_width : q_width + kv_width] = w_keyval[0].astype(BF16)
     q_shard[:, q_width + kv_width : qkv_width] = w_keyval[1].astype(BF16)
     o_shard[...] = w_out[...].astype(BF16)
-    cos[:block, :] = jnp.zeros((block, LANES), F32)
-    cos[:block, :experts] = w_router[...]
-    value = jnp.concatenate([gains[...], jnp.zeros((LANES - 2, block), F32)]).T
-    value = value + pltpu.roll(cos[:block, :], 2, 1)
+    value = jnp.concatenate(
+        [gains[...], w_router[...], jnp.zeros((LANES - each, block), F32)]
+    ).T
     high = value.astype(BF16).astype(F32)
     mid = (value - high).astype(BF16).astype(F32)
     low = value - high - mid
@@ -1961,81 +1743,6 @@
     )(*values, *earlier)
 
 
-def fence_kernel(*refs):
-    count = len(refs) // 2
-    for value, out in zip(refs[:count], refs[count:]):
-        out[...] = value[...]
-
-
-def fence_all(values, *earlier):
-    return whole_call(fence_kernel, values, [(v.shape, v.dtype) for v in values], earlier, "fence")
-
-
-def fence(value, *earlier):
-    return fence_all([value], *earlier)[0]
-
-
-def sum_y_kernel(near, got, *outs):
-    for k, out in enumerate(outs):
-        out[...] = (near[k].astype(F32) + got[k].astype(F32)).astype(BF16)
-
-
-def sum_y(near, got, *earlier):
-    outs = [(near.shape[1:], BF16)] * SLOTS
-    return whole_call(sum_y_kernel, [near, got], outs, earlier, "sum_y")
-
-
-def sum_z_kernel(x_at, *refs):
-    kept, given = refs[-2:]
-    half = kept.shape[1]
-    for c in range(kept.shape[0]):
-        parts = refs[SLOTS * c : SLOTS * (c + 1)]
-        for rows, out in ((x_at[0], kept), (1 - x_at[0], given)):
-            rows = pl.ds(pl.multiple_of(rows * half, half), half)
-            total = parts[0][rows, :].astype(F32)
-            for part in parts[1:]:
-                total = total + part[rows, :].astype(F32)
-            out[c] = total.astype(out.dtype)
-
-
-def sum_z(x_at, chunks, *earlier):
-    count = len(chunks)
-    pair, columns = chunks[0][0].shape
-    flat = [part for parts in chunks for part in parts]
-    return pl.pallas_call(
-        with_earlier(sum_z_kernel, 1 + len(flat), len(earlier)),
-        in_specs=[smem_spec()] + [vmem_spec()] * len(flat) + any_specs(earlier),
-        out_specs=[vmem_spec()] * 2,
-        out_shape=[
-            jax.ShapeDtypeStruct((count, pair // 2, columns), F32),
-            jax.ShapeDtypeStruct((count, pair // 2, columns), BF16),
-        ],
-        compiler_params=pltpu.CompilerParams(vmem_limit_bytes=VMEM_BYTES),
-        name="sum_z",
-    )(x_at, *flat, *earlier)
-
-
-def sum_parts_kernel(parts, out):
-    total = parts[0].astype(F32)
-    for c in range(1, parts.shape[0]):
-        total = total + parts[c].astype(F32)
-    out[...] = total.astype(BF16)
-
-
-def sum_parts(parts, *earlier):
-    chunks, tokens, width = parts.shape
-    return pl.pallas_call(
-        with_earlier(sum_parts_kernel, 1, len(earlier)),
-        grid=(tokens // EXPERT_ROWS,),
-        in_specs=[pl.BlockSpec((chunks, EXPERT_ROWS, width), lambda s: (0, s, 0))]
-        + any_specs(earlier),
-        out_specs=pl.BlockSpec((EXPERT_ROWS, width), lambda s: (s, 0)),
-        out_shape=jax.ShapeDtypeStruct((tokens, width), BF16),
-        compiler_params=pltpu.CompilerParams(vmem_limit_bytes=VMEM_BYTES),
-        name="sum_parts",
-    )(parts, *earlier)
-
-
 def adam_attention_kernel(q_share, o_share, *refs):
     states, outs = refs[:9], refs[9:18]
     gain_part = refs[18]
@@ -2112,39 +1819,6 @@
     )(x_at, kept, got, *gateup, *down)
 
 
-def join_tokens_kernel(own, first, second, out, turned):
-    half = own.shape[0] // 2
-    for at, part in ((0, own[:half, :]), (half, own[half:, :]), (2 * half, first[...]), (3 * half, second[...])):
-        out[at : at + half, :] = part
-        turned[:, at : at + half] = part.T
-
-
-def join_tokens(own, first, second, *earlier):
-    tokens, width = own.shape
-    return pl.pallas_call(
-        with_earlier(join_tokens_kernel, 3, len(earlier)),
-        in_specs=[vmem_spec()] * 3 + any_specs(earlier),
-        out_specs=[vmem_spec()] * 2,
-        out_shape=[
-            jax.ShapeDtypeStruct((2 * tokens, width), own.dtype),
-            jax.ShapeDtypeStruct((width, 2 * tokens), own.dtype),
-        ],
-        compiler_params=pltpu.CompilerParams(vmem_limit_bytes=VMEM_BYTES),
-        name="join_tokens",
-    )(own, first, second, *earlier)
-
-
-def move(array, dz=0, dy=0, dx=0):
-    total = lax.axis_size("dp")
-    inner = total // 16
-    pairs = []
-    for at in range(16):
-        z, y, x = at // 4, at // 2 % 2, at % 2
-        to = ((z + dz) % 4) * 4 + (y ^ dy) * 2 + (x ^ dx)
-        pairs += [(at * inner + i, to * inner + i) for i in range(inner)]
-    return lax.ppermute(array, "dp", pairs)
-
-
 def place():
     at = lax.axis_index("dp") // (lax.axis_size("dp") // 16)
     return at // 4, at // 2 % 2, at % 2
@@ -2173,92 +1847,6 @@
     )
 
 
-def block_rows(parts, rows):
-    z, y, x = place()
-    starts = []
-    for dz, dy, dx in parts:
-        starts.append((((z + dz + 4) % 4) * 4 + (y ^ dy) * 2 + (x ^ dx)) * rows)
-    return jnp.stack(starts).astype(jnp.int32)
-
-
-def gather_z(shard):
-    return jnp.stack([shard] + [move(shard, dz=-dz) for dz in Z_FROM[1:]])
-
-
-def gather_ring(shard):
-    below, above = move(shard, dz=1), move(shard, dz=-1)
-    return [shard, below, above, move(below, dz=1)]
-
-
-def send_z(parts):
-    return [move(parts[k].astype(BF16), dz=Z_FROM[k]) for k in range(1, SLOTS)]
-
-
-def scatter_z(parts, moved=None):
-    result = parts[0]
-    for one in moved or send_z(parts):
-        result = result + one.astype(F32)
-    return result
-
-
-def gather_plane(own):
-    half = own.shape[-1] // 2
-    along_y, along_x = move(own, dy=1), move(own, dx=1)
-    both = (move(along_y[..., :half], dx=1), move(along_x[..., half:], dy=1))
-    return own, along_y, along_x, *both
-
-
-def scatter_plane(pieces):
-    own, along_y, along_x, both_one, both_two = pieces
-    half = both_one.shape[-1]
-    got_one, got_two = move(both_one, dx=1), move(both_two, dy=1)
-    pass_y = jnp.concatenate(
-        [(along_y[..., :half].astype(F32) + got_one.astype(F32)).astype(BF16), along_y[..., half:]],
-        axis=-1,
-    )
-    pass_x = jnp.concatenate(
-        [along_x[..., :half], (along_x[..., half:].astype(F32) + got_two.astype(F32)).astype(BF16)],
-        axis=-1,
-    )
-    got_y, got_x = move(pass_y, dy=1), move(pass_x, dx=1)
-    return scatter_z(
-        [
-            own[k].astype(F32) + got_y[k].astype(F32) + got_x[k].astype(F32)
-            for k in range(SLOTS)
-        ]
-    )
-
-
-PLANE = [(dz, dy, dx) for dy, dx in ((0, 0), (1, 0), (0, 1), (1, 1)) for dz in Z_FROM]
-
-
-def join_kernel(rows_at, *refs):
-    pieces, out = refs[:-1], refs[-1]
-    slots, own, width = pieces[0].shape
-    half = width // 2
-    for at in range(4 * slots):
-        rows = pl.ds(pl.multiple_of(rows_at[at], own), own)
-        group, slot = at // slots, at % slots
-        if group < 3:
-            out[rows, :] = pieces[group][slot]
-        else:
-            out[rows, :half] = pieces[3][slot]
-            out[rows, half:] = pieces[4][slot]
-
-
-def part_kernel(rows_at, whole, *pieces):
-    slots, own, width = pieces[0].shape
-    half = width // 2
-    for at in range(4 * slots):
-        rows = pl.ds(pl.multiple_of(rows_at[at], own), own)
-        group, slot = at // slots, at % slots
-        if group < 3:
-            pieces[group][slot] = whole[rows, :]
-        else:
-            pieces[3][slot] = whole[rows, :half]
-            pieces[4][slot] = whole[rows, half:]
-
-
 def smem_spec():
     return pl.BlockSpec(memory_space=pltpu.SMEM)
 
@@ -2267,62 +1855,12 @@
     return pl.BlockSpec(memory_space=pltpu.VMEM)
 
 
-def join_blocks(rows_at, pieces, earlier=()):
-    slots, own, width = pieces[0].shape
-    return pl.pallas_call(
-        with_earlier(join_kernel, 6, len(earlier)),
-        in_specs=[smem_spec()] + [vmem_spec()] * 5 + any_specs(earlier),
-        out_specs=vmem_spec(),
-        out_shape=jax.ShapeDtypeStruct((4 * slots * own, width), BF16),
-        compiler_params=pltpu.CompilerParams(vmem_limit_bytes=VMEM_BYTES),
-        name="join_blocks",
-    )(rows_at, *pieces, *earlier)
-
-
-def part_blocks(rows_at, whole, earlier=()):
-    own, width = whole.shape[0] // (4 * SLOTS), whole.shape[1]
-    full = jax.ShapeDtypeStruct((SLOTS, own, width), BF16)
-    half = jax.ShapeDtypeStruct((SLOTS, own, width // 2), BF16)
-    return pl.pallas_call(
-        with_earlier(part_kernel, 2, len(earlier)),
-        in_specs=[smem_spec(), vmem_spec()] + any_specs(earlier),
-        out_specs=[vmem_spec()] * 5,
-        out_shape=[full] * 3 + [half] * 2,
-        compiler_params=pltpu.CompilerParams(vmem_limit_bytes=VMEM_BYTES),
-        name="part_blocks",
-    )(rows_at, whole, *earlier)
-
-
-def after(value, *earlier):
-    marks = []
-    for one in earlier:
-        slots = one.shape[0] if one.shape[0] == SLOTS else 1
-        lead, rest = (slots > 1) * 1, one.ndim - 1
-        marks.append(lax.slice(one, (lead,) + (0,) * rest, (slots,) + (1,) * rest))
-    return lax.optimization_barrier((value, *marks))[0]
-
-
-def split_three(values):
-    high = values.astype(BF16)
-    rest = values - high.astype(F32)
-    middle = rest.astype(BF16)
-    low = (rest - middle.astype(F32)).astype(BF16)
-    return [high, middle, low]
-
-
 def swap_cores(part):
     return lax.ppermute(part, "tensor", [(0, 1), (1, 0)])
 
 
 def pair_sum(part):
     return part.astype(F32) + swap_cores(part).astype(F32)
-
-
-def norm_backward(values, inverse, gain_row, upstream):
-    scaled = values * inverse
-    weighted = upstream * gain_row
-    mean_term = jnp.mean(weighted * scaled, axis=-1, keepdims=True)
-    return (inverse * (weighted - scaled * mean_term), jnp.sum(upstream * scaled, axis=0))
 
 
 def adam_update(value, gradient, mean_old, square_old, rate, decay):
@@ -2361,31 +1899,23 @@
     down_mean,
     down_square,
 ):
-    tokens, width = hidden_in.shape
-    own = w_query.shape[0]
-    experts, hidden = w_down.shape[0], w_down.shape[1]
+    experts = w_down.shape[0]
     q_width, kv_width = w_query.shape[1], key_value_weight.shape[2]
     qkv_width = q_width + 2 * kv_width
-    each = 2 + experts
-    half_experts = experts // 2
-    block = width // 16
-    z_at, y_at, x_at = place()
-    core = lax.axis_index("tensor")
-    plane_rows = block_rows(PLANE, block)
+    x_at = lax.axis_index("dp") // (lax.axis_size("dp") // 16) % 2
     turned_down = [one.transpose(0, 2, 1) for one in (w_down, down_mean, down_square)]
     gateup_rows, down_rows = w_gateup, turned_down[0]
     if lax.axis_size("dp") > 16:
         gateup_rows = inner_gather(w_gateup.astype(BF16), 2)
         down_rows = inner_gather(down_rows.astype(BF16), 1)
-    chunks = experts // (2 * CHUNK)
-    first = x_at == 0
     half_width = HEAD_DIM // 2
     frequency = ROPE_BASE ** (-2.0 * jnp.arange(half_width, dtype=F32) / HEAD_DIM)
     frequency = jnp.concatenate([frequency] * 4)[None, :]
     turned_out = [one.T for one in (w_out, out_mean, out_square)]
+    turned_router = [one.T for one in (w_router, router_mean, router_square)]
     weights = (
         inner_gather(w_query, 0), inner_gather(key_value_weight, 1),
-        inner_gather(turned_out[0], 0), inner_gather(w_router, 0), inner_gather(norm_gains, 1),
+        inner_gather(turned_out[0], 0), inner_gather(turned_router[0], 1), inner_gather(norm_gains, 1),
     )
     (
         small, combine, combine_pair, seg_col,
@@ -2415,11 +1945,12 @@
     )
     gain_one_share = pair_sum(gain_one_part.T) / norm_gains[:1]
     gains_share = jnp.concatenate([gain_one_share, qkv_share[:, qkv_width][None, :]])
-    router_share = qkv_share[:, qkv_width + 1 : qkv_width + 1 + experts]
+    router_share = qkv_share[:, qkv_width + 1 : qkv_width + 1 + experts].T
 
     gains_result = adam_update(norm_gains, gains_share, gains_mean, gains_square, GAIN_RATE, 0.0)
     router_result = adam_update(
-        w_router, router_share, router_mean, router_square, (4 * MODEL_DIM) ** (-0.5), WEIGHT_DECAY
+        turned_router[0], router_share, turned_router[1], turned_router[2],
+        (4 * MODEL_DIM) ** (-0.5), WEIGHT_DECAY,
     )
     expert_results = adam_experts(
         x_here, kept_share, got_share,
@@ -2431,7 +1962,7 @@
         + gains_result
         + tuple(attention_results[:6])
         + tuple(one.T for one in attention_results[6:])
-        + router_result
+        + tuple(one.T for one in router_result)
         + tuple(expert_results)
     )
 

time: 625 us -> 624 us (level)
  no operation moved by 1% of the time
where the time goes in v3:
time: 624 us; the launch traced here: 615 us
  Pallas kernels  591 us (95%)
  local copies, waits for them, and re-layouts  10.9 us (2%)
  starting transfers between devices  9.42 us (2%)
    pallas_call x1, Pallas kernels, experts_pass(): pl.pallas_call(functools.partial(experts_kernel, inner, chunks, row_steps...  211 us
    pallas_call x1, Pallas kernels, forward_pass(): pl.pallas_call(functools.partial(forward_kernel, inner), in_specs=[vmem]...  185 us
    pallas_call x1, Pallas kernels, backward_pass(): pl.pallas_call(functools.partial(backward_kernel, inner), in_specs=[vmem]...  176 us
    pallas_call x1, Pallas kernels, adam_experts(): pl.pallas_call(adam_experts_kernel, grid=(experts // CHUNK,), in_specs=[s...  15.1 us
  transfers between devices with their start and end apart: 1, of which 0 were waited for; matrix products, arithmetic and copies ran while one was open for 1% of the time, Pallas kernels for 2%

profile of v3, /device:TPU:3, one launch (start us, length us, event | category | flops | bytes accessed | tf_op | source)
XLA Modules:
  0.0 615.4 jit_solution(16362310691770183121)
XLA Ops:
  0.7 0.6 maximum_bitcast_fusion.frequency
  1.3 185.1 %forward_pass.1 = (f32[24,1536]{1,0:T(8,128)}, f32[1024,128]{1,0:T(8,128)}, f32[2048,8]{1,0:T(8,128)}, f32[1024,1]{1,0:T(8,128)}, bf16[16,96,1408]{2,1,0:T(8,128...) custom-call(f32[96,768]{1,0:T(8,128)} %refs_2_.2, ...), custom_call_target="tpu_custom_call" | custom-call | tf_op jit(solution)/shard_map/forward_pass/pallas_call | solution.py:1068
  186.4 211.3 %experts_pass.1 = (bf16[1024,1536]{1,0:T(8,128)(2,1)}, bf16[1024,1536]{1,0:T(8,128)(2,1)}, bf16[1024,1536]{1,0:T(8,128)(2,1)}, bf16[2048,1536]{1,0:T(8,128)(2,1)...) custom-call(bf16[2048,1536]{1,0:T(8,128)(2,1)} %get-tuple-element.84, ...), custom_call_target="tpu_custom_call" | custom-call | flops 154618822656 | bytes 18874368 | tf_op jit(solution)/shard_map/experts_pass/pallas_call | solution.py:425
  397.7 175.8 %backward_pass.1 = (f32[96,1408]{1,0:T(8,128)}, f32[96,768]{1,0:T(8,128)}, f32[1024,1536]{1,0:T(8,128)}, bf16[1024,1536]{1,0:T(8,128)(2,1)}, f32[4,96,1536]{2,1,...) custom-call(f32[1024,1]{1,0:T(8,128)} %get-tuple-element.81.seg_col,, ...), custom_call_target="tpu_custom_call" | custom-call | tf_op jit(solution)/shard_map/backward_pass/pallas_call | solution.py:1684
  573.4 0.0 copy-start.1
  573.4 0.0 copy-start.2
  573.4 0.0 copy-start.3
  573.5 3.7 adam_attention.1
  577.2 0.9 reduce
  578.1 9.4 %collective-permute-start = (f32[1,96]{1,0:T(1,128)S(1)}, f32[1,96]{1,0:T(1,128)S(1)}, u32[]{:S(2)}, u32[]{:S(2)}) collective-permute-start(f32[1,96]{1,0:T(1,128)S(1)} %bitcast.34), channel_id=1, source_target_pairs={{0,1},{1,0},{2,3},{3,2},{4,5},{5,4},{6,7},{7,6},{8,9},{9,8},{10,11... | collective-permute-start | bytes 1160 | tf_op jit(solution)/shard_map/ppermute | solution.py:1859
  587.5 0.9 slice_reduce_fusion
  588.4 0.0 copy-done.1
  588.4 0.1 copy.72
  588.5 0.0 copy-done.2
  588.5 0.1 copy.69
  588.6 0.0 copy-done.3
  588.7 0.1 copy.70
  588.7 0.1 copy.71
  588.8 0.9 multiply_subtract_fusion
  589.8 0.7 copy.73
  590.4 0.7 copy.74
  591.1 0.7 copy.75
  591.8 0.0 copy-start.4
  591.8 0.0 copy-start.5
  591.8 0.0 copy-start.6
  591.8 0.0 copy-start
  591.8 15.1 %adam_experts.1 = (f32[16,2,96,256]{3,2,1,0:T(8,128)}, f32[16,2,96,256]{3,2,1,0:T(8,128)}, f32[16,2,96,256]{3,2,1,0:T(8,128)}, f32[16,96,256]{2,1,0:T(8,128)}, f...) custom-call(s32[1]{0:T(128)} %bitcast.11.x_at, f32[4,96,1536]{2,1,0:T(8,128)} %get-tuple-element.131.kept, ...), custom_call_target="tpu_custom_call" | custom-call | tf_op jit(solution)/shard_map/adam_experts/pallas_call | solution.py:1810
  606.9 0.0 collective-permute-done
  606.9 0.0 copy-done.4
  606.9 0.0 copy-done.5
  606.9 0.0 copy-done.6
  606.9 0.6 multiply_subtract_fusion.1
  607.5 0.0 copy-done
  607.5 1.7 copy.78
  609.2 5.9 copy.79
  (5 shorter events, 0.0 us)
Async XLA Ops:
  573.4 15.0 %copy-start.1 = (f32[96,16]{0,1:T(8,128)S(1)}, f32[96,16]{0,1:T(8,128)}, u32[]{:S(2)}) copy-start(f32[96,16]{0,1:T(8,128)} %param.41) | copy-start | bytes 18436
  573.4 15.1 %copy-start.2 = (f32[96,16]{0,1:T(8,128)S(1)}, f32[96,16]{0,1:T(8,128)}, u32[]{:S(2)}) copy-start(f32[96,16]{0,1:T(8,128)} %param.42) | copy-start | bytes 18436
  573.4 15.2 %copy-start.3 = (f32[96,16]{0,1:T(8,128)S(1)}, f32[96,16]{0,1:T(8,128)}, u32[]{:S(2)}) copy-start(f32[96,16]{0,1:T(8,128)} %param.43) | copy-start | bytes 18436
  578.1 28.8 %collective-permute-start = (f32[1,96]{1,0:T(1,128)S(1)}, f32[1,96]{1,0:T(1,128)S(1)}, u32[]{:S(2)}, u32[]{:S(2)}) collective-permute-start(f32[1,96]{1,0:T(1,128)S(1)} %bitcast.34), channel_id=1, source_target_pairs={{0,1},{1,0},{2,3},{3,2},{4,5},{5,4},{6,7},{7,6},{8,9},{9,8},{10,11... | collective-permute-start | bytes 1160 | tf_op jit(solution)/shard_map/ppermute | solution.py:1859
  591.8 15.1 %copy-start.4 = (f32[2,96]{1,0:T(2,128)S(1)}, f32[2,96]{1,0:T(2,128)}, u32[]{:S(2)}) copy-start(f32[2,96]{1,0:T(2,128)} %gains.1) | copy-start | bytes 2308
  591.8 15.2 %copy-start.5 = (f32[2,96]{1,0:T(2,128)S(1)}, f32[2,96]{1,0:T(2,128)}, u32[]{:S(2)}) copy-start(f32[2,96]{1,0:T(2,128)} %param.31) | copy-start | bytes 2308
  591.8 15.2 %copy-start.6 = (f32[2,96]{1,0:T(2,128)S(1)}, f32[2,96]{1,0:T(2,128)}, u32[]{:S(2)}) copy-start(f32[2,96]{1,0:T(2,128)} %param.30) | copy-start | bytes 2308
  591.8 15.8 %copy-start = (bf16[1024,1536]{1,0:T(8,128)(2,1)S(1)}, bf16[1024,1536]{1,0:T(8,128)(2,1)}, u32[]{:S(2)}) copy-start(bf16[1024,1536]{1,0:T(8,128)(2,1)} %get-tuple-element.237) | copy-start | bytes 9437188
